TPU v7x, 32 devices: a whole 2x2x4 slice. The times are simulated.
32 devices in a mesh: dp: 8 (over z, x), tensor: 4 (over y, core).
Axes of the slice: x: 2, y: 2, z: 4, core: 2. Of those that a mesh axis runs over, the one named last changes fastest.
Arguments:
- tokens: bfloat16 [8192, 768], P('dp'), may hold values from -6 to 6
- first_gain: float32 [768], replicated, may hold values from 0.1 to 1.9
- joint_weight: bfloat16 [768, 3, 768], P(None, None, 'tensor'), may hold values from -0.21875 to 0.21875
- output_weight: bfloat16 [768, 768], P('tensor'), may hold values from -4 to 4
- second_gain: float32 [768], replicated, may hold values from 0.1 to 1.9
- expand_weight: bfloat16 [768, 2, 1152], P(None, None, 'tensor'), may hold values from -0.21875 to 0.21875
- shrink_weight: bfloat16 [1152, 768], P('tensor'), may hold values from -0.1875 to 0.1875
- cotangent: bfloat16 [8192, 768], P(('dp', 'tensor')), may hold values from -6 to 6
Outputs:
- block_out: bfloat16 [8192, 768], P(('dp', 'tensor'))
- grad_tokens: float32 [8192, 768], P(('dp', 'tensor'))
- grad_first_gain: float32 [768], replicated
- grad_joint_weight: float32 [768, 3, 768], P(None, None, 'tensor')
- grad_output_weight: float32 [768, 768], P('tensor')
- grad_second_gain: float32 [768], replicated
- grad_expand_weight: float32 [768, 2, 1152], P(None, None, 'tensor')
- grad_shrink_weight: float32 [1152, 768], P('tensor')
All inputs are finite; a program needn't handle non-finite values.
Results may differ from a plain program's by a relative error of at most 0.025.
Values may be sent and summed in bfloat16 or wider, within the bound.
A program may use at most 128 MiB of HBM per device.

v0:
```python
import jax
import jax.numpy as jnp
from jax import lax
from jax.sharding import PartitionSpec as P

HEAD_DIM = 64
SEQ_LEN = 1024


eps_norm = 1e-05
theta_base = 160000.0


def layer_norm(values, gain_vector):
    centred = values - jnp.mean(values, axis=-1, keepdims=True)
    spread = jnp.mean(centred * centred, axis=-1, keepdims=True)
    return centred * lax.rsqrt(spread + eps_norm) * gain_vector


def rotary_tables(seq_length, head_width):
    half_width = head_width // 2
    frequency = theta_base ** (-(jnp.arange(half_width, dtype=jnp.float32) * 2.0 / head_width))
    angles = jnp.arange(seq_length, dtype=jnp.float32)[:, None] * frequency[None, :]
    angles = jnp.concatenate([angles, angles], axis=1)
    return (jnp.cos(angles), jnp.sin(angles))


def rotate(values, cosine, sine_table):
    half_width = values.shape[-1] // 2
    turned = jnp.concatenate([-values[..., half_width:], values[..., :half_width]], axis=-1)
    return values * cosine[:, None, :] + turned * sine_table[:, None, :]


def on_device(
    tokens,
    first_gain,
    joint_weight,
    output_weight,
    second_gain,
    expand_weight,
    shrink_weight,
    cotangent,
):
    local_rows, model_width = tokens.shape
    group_size = lax.axis_size("tensor")
    own_rows = local_rows // group_size
    row_offset = lax.axis_index("tensor") * own_rows
    heads_here = joint_weight.shape[2] // HEAD_DIM
    inner_width = heads_here * HEAD_DIM
    unit_count = expand_weight.shape[2]
    seq_length = SEQ_LEN
    block_rows = min(512, seq_length)
    blocks_per_seq = seq_length // block_rows
    block_count = local_rows // block_rows
    score_scale = HEAD_DIM ** (-0.5)
    joint_flat = joint_weight.reshape(model_width, 3 * inner_width)
    expand_flat = expand_weight.reshape(model_width, 2 * unit_count)
    float_tokens = tokens.astype(jnp.float32)
    normed = layer_norm(float_tokens, first_gain).astype(jnp.bfloat16)
    joint_out = jnp.dot(normed, joint_flat, preferred_element_type=jnp.float32)
    joint_out = joint_out.reshape(local_rows, 3, heads_here, HEAD_DIM)
    cosine, sine_table = rotary_tables(seq_length, HEAD_DIM)
    cosine_all = jnp.tile(cosine, (local_rows // seq_length, 1))
    sine_all = jnp.tile(sine_table, (local_rows // seq_length, 1))

    def turn(values):
        return rotate(values, cosine_all, sine_all)

    query_rot, turn_back = jax.vjp(turn, joint_out[:, 0])
    query_rot = query_rot.astype(jnp.bfloat16)
    key_rot = turn(joint_out[:, 1]).astype(jnp.bfloat16)
    value_rows = joint_out[:, 2].astype(jnp.bfloat16)

    def block_slices(block_index):
        row_start = block_index * block_rows
        seq_start = block_index // blocks_per_seq * seq_length
        query_block = lax.dynamic_slice_in_dim(query_rot, row_start, block_rows, 0)
        return (row_start, seq_start, query_block, key_rot, value_rows)

    def attend(block_index):
        row_start, seq_start, query_block, key_seq, value_seq = block_slices(block_index)
        scores = (
            jnp.einsum("qhd,khd->hqk", query_block, key_seq, preferred_element_type=jnp.float32)
            * score_scale
        )
        row_peak = jnp.max(scores, axis=-1, keepdims=True)
        exp_scores = jnp.exp(scores - row_peak)
        row_total = jnp.sum(exp_scores, axis=-1, keepdims=True)
        prob_block = (exp_scores / row_total).astype(jnp.bfloat16)
        mixed_block = jnp.einsum(
            "hqk,khd->qhd", prob_block, value_seq, preferred_element_type=jnp.float32
        )
        return (mixed_block, (row_peak + jnp.log(row_total))[..., 0])

    block_ids = jnp.arange(block_count, dtype=jnp.int32)
    mixed_blocks, logsum = lax.map(attend, block_ids)
    mixed_low = mixed_blocks.reshape(local_rows, inner_width).astype(jnp.bfloat16)
    branch_part = jnp.dot(mixed_low, output_weight, preferred_element_type=jnp.float32)
    branch = lax.psum_scatter(
        branch_part.astype(jnp.bfloat16), "tensor", scatter_dimension=0, tiled=True
    ).astype(jnp.float32)
    own_tokens = lax.dynamic_slice_in_dim(float_tokens, row_offset, own_rows, 0)
    middle = own_tokens + branch
    second_own = layer_norm(middle, second_gain).astype(jnp.bfloat16)
    second = lax.all_gather(second_own, "tensor", axis=0, tiled=True)
    gate_up = jnp.dot(second, expand_flat, preferred_element_type=jnp.float32)
    gate_up = gate_up.reshape(local_rows, 2, unit_count)

    def activate(gate_part, up_part):
        return jax.nn.gelu(gate_part, approximate=True) * up_part

    hidden, activate_back = jax.vjp(activate, gate_up[:, 0], gate_up[:, 1])
    hidden_low = hidden.astype(jnp.bfloat16)
    shrink_part = jnp.dot(hidden_low, shrink_weight, preferred_element_type=jnp.float32)
    shrink_total = lax.psum_scatter(
        shrink_part.astype(jnp.bfloat16), "tensor", scatter_dimension=0, tiled=True
    ).astype(jnp.float32)
    block_out = (middle + shrink_total).astype(jnp.bfloat16)
    grad_rows = lax.all_gather(cotangent, "tensor", axis=0, tiled=True)
    grad_shrink = jnp.einsum("tu,td->ud", hidden_low, grad_rows, preferred_element_type=jnp.float32)
    grad_hidden = jnp.einsum(
        "td,ud->tu", grad_rows, shrink_weight, preferred_element_type=jnp.float32
    )
    grad_gate, grad_up = activate_back(grad_hidden)
    grad_both = (
        jnp.stack([grad_gate, grad_up], axis=1)
        .astype(jnp.bfloat16)
        .reshape(local_rows, 2 * unit_count)
    )
    grad_expand = jnp.einsum("td,tu->du", second, grad_both, preferred_element_type=jnp.float32)
    grad_expand = grad_expand.reshape(model_width, 2, unit_count)
    second_part = jnp.einsum(
        "tu,du->td", grad_both, expand_flat, preferred_element_type=jnp.float32
    )
    grad_second = lax.psum_scatter(
        second_part.astype(jnp.bfloat16), "tensor", scatter_dimension=0, tiled=True
    ).astype(jnp.float32)
    _, second_back = jax.vjp(layer_norm, middle, second_gain)
    grad_middle_norm, gain_two_part = second_back(grad_second)
    grad_middle = cotangent.astype(jnp.float32) + grad_middle_norm
    grad_branch = lax.all_gather(grad_middle.astype(jnp.bfloat16), "tensor", axis=0, tiled=True)
    grad_output = jnp.einsum(
        "ti,td->id", mixed_low, grad_branch, preferred_element_type=jnp.float32
    )
    grad_mixed = jnp.einsum(
        "td,id->ti", grad_branch, output_weight, preferred_element_type=jnp.float32
    )
    grad_mixed = grad_mixed.astype(jnp.bfloat16).reshape(local_rows, heads_here, HEAD_DIM)

    def attend_back(carried, inputs):
        grad_keys, grad_values = carried
        block_index, block_logsum = inputs
        row_start, seq_start, query_block, key_seq, value_seq = block_slices(block_index)
        grad_block = lax.dynamic_slice_in_dim(grad_mixed, row_start, block_rows, 0)
        scores = (
            jnp.einsum("qhd,khd->hqk", query_block, key_seq, preferred_element_type=jnp.float32)
            * score_scale
        )
        prob_block = jnp.exp(scores - block_logsum[..., None])
        grad_probs = jnp.einsum(
            "qhd,khd->hqk", grad_block, value_seq, preferred_element_type=jnp.float32
        )
        row_delta = jnp.sum(prob_block * grad_probs, axis=-1, keepdims=True)
        grad_scores = (prob_block * (grad_probs - row_delta)).astype(jnp.bfloat16)
        grad_query = (
            jnp.einsum("hqk,khd->qhd", grad_scores, key_seq, preferred_element_type=jnp.float32)
            * score_scale
        )
        key_part = (
            jnp.einsum("hqk,qhd->khd", grad_scores, query_block, preferred_element_type=jnp.float32)
            * score_scale
        )
        value_part = jnp.einsum(
            "hqk,qhd->khd",
            prob_block.astype(jnp.bfloat16),
            grad_block,
            preferred_element_type=jnp.float32,
        )
        key_now = grad_keys
        value_now = grad_values
        grad_keys = key_now + key_part
        grad_values = value_now + value_part
        return ((grad_keys, grad_values), grad_query)

    empty_grad = jnp.zeros((local_rows, heads_here, HEAD_DIM), jnp.float32)
    (grad_keys, grad_values), grad_queries = lax.scan(
        attend_back, (empty_grad, empty_grad), (block_ids, logsum)
    )
    grad_queries = grad_queries.reshape(local_rows, heads_here, HEAD_DIM)
    grad_query_raw = turn_back(grad_queries)[0]
    grad_key_raw = turn_back(grad_keys)[0]
    grad_joint = jnp.stack([grad_query_raw, grad_key_raw, grad_values], axis=1)
    grad_joint = grad_joint.astype(jnp.bfloat16).reshape(local_rows, 3 * inner_width)
    grad_joint_w = jnp.einsum("td,tj->dj", normed, grad_joint, preferred_element_type=jnp.float32)
    grad_joint_w = grad_joint_w.reshape(model_width, 3, inner_width)
    first_part = jnp.einsum("tj,dj->td", grad_joint, joint_flat, preferred_element_type=jnp.float32)
    grad_first = lax.psum_scatter(
        first_part.astype(jnp.bfloat16), "tensor", scatter_dimension=0, tiled=True
    ).astype(jnp.float32)
    _, first_back = jax.vjp(layer_norm, own_tokens, first_gain)
    grad_norm_in, gain_one_part = first_back(grad_first)
    grad_tokens = grad_middle + grad_norm_in
    gain_one, gain_two = lax.psum((gain_one_part, gain_two_part), ("dp", "tensor"))
    grad_joint_w, grad_output, grad_expand, grad_shrink = lax.psum(
        (grad_joint_w, grad_output, grad_expand, grad_shrink), "dp"
    )
    return (
        block_out,
        grad_tokens,
        gain_one,
        grad_joint_w,
        grad_output,
        gain_two,
        grad_expand,
        grad_shrink,
    )


def solution(mesh):
    return jax.shard_map(
        on_device,
        mesh=mesh,
        in_specs=(
            P("dp", None),
            P(),
            P(None, None, "tensor"),
            P("tensor", None),
            P(),
            P(None, None, "tensor"),
            P("tensor", None),
            P(("dp", "tensor"), None),
        ),
        out_specs=(
            P(("dp", "tensor"), None),
            P(("dp", "tensor"), None),
            P(),
            P(None, None, "tensor"),
            P("tensor", None),
            P(),
            P(None, None, "tensor"),
            P("tensor", None),
        ),
        check_vma=False,
    )
```

profile of v0, /device:TPU:0, one launch (start us, length us, event | category | flops | bytes accessed | tf_op | source)
XLA Modules:
  0.0 473.0 jit_solution(1444229949902726733)
XLA Ops:
  7.3 1.8 convert_reduce_fusion
  9.9 1.3 fusion.33
  11.3 1.4 copy-done.5
  16.2 11.1 %while.27 = (s32[]{:T(128)}, bf16[2,512,3,64]{1,3,2,0:T(8,128)(2,1)S(1)}, f32[2,3,512]{2,1,0:T(4,128)S(1)}, s32[2]{0:T(128)S(1)}, bf16[1024,3,64]{0,2,1:T(8,128)...) while((s32[]{:T(128)}, ...), condition=%wide.region_5.6_spmd, body=%wide.region_2.5_spmd.sunk | while | flops 416807424 | bytes 20310204 | solution.py:96
  18.5 1.3 fusion.120
  19.9 1.8 fusion.121
  24.1 1.3 fusion.120
  25.4 1.8 fusion.121
  28.5 1.8 convolution_convert_fusion.2
  30.3 3.3 convert_element_type.94
  33.6 27.7 %reduce-scatter.5.cloned.1.call-done = bf16[256,768]{1,0:T(8,128)(2,1)} async-done(((bf16[1024,768]{1,0:T(8,128)(2,1)}), bf16[256,768]{1,0:T(8,128)(2,1)}) %reduce-scatter.5.cloned.1.call-update) | async-done | bytes 393232 | tf_op jit(solution)/shard_map/reduce_scatter | solution.py:99
  61.3 2.0 fusion.72
  65.5 18.9 %all-gather.4.cloned.1.call-done = bf16[1024,768]{1,0:T(8,128)(2,1)} async-done(((bf16[256,768]{1,0:T(8,128)(2,1)}), bf16[1024,768]{1,0:T(8,128)(2,1)}) %all-gather.4.cloned.1.call-update) | async-done | bytes 1572880 | tf_op jit(solution)/shard_map/all_gather | solution.py:105
  84.4 4.2 fusion.39
  88.5 17.2 %all-gather.6.cloned.1.call-done = bf16[1024,768]{1,0:T(8,128)(2,1)} async-done(((bf16[256,768]{1,0:T(8,128)(2,1)}), bf16[1024,768]{1,0:T(8,128)(2,1)}) %all-gather.6.cloned.1.call-update) | async-done | bytes 1572880 | tf_op jit(solution)/shard_map/all_gather | solution.py:119
  105.7 3.6 fusion.47
  110.4 2.6 bitcast_convert_fusion
  113.0 2.1 multiply_convert_fusion.2
  116.0 2.2 convolution_convert_fusion.1
  118.2 23.1 %reduce-scatter.9.cloned.1.call-done = bf16[256,768]{1,0:T(8,128)(2,1)} async-done(((bf16[1024,768]{1,0:T(8,128)(2,1)}), bf16[256,768]{1,0:T(8,128)(2,1)}) %reduce-scatter.9.cloned.1.call-update) | async-done | bytes 393232 | tf_op jit(solution)/shard_map/reduce_scatter | solution.py:135
  141.3 2.0 fusion.56
  144.6 27.9 %reduce-scatter.7.cloned.1.call-done = bf16[256,768]{1,0:T(8,128)(2,1)} async-done(((bf16[1024,768]{1,0:T(8,128)(2,1)}), bf16[256,768]{1,0:T(8,128)(2,1)}) %reduce-scatter.7.cloned.1.call-update) | async-done | bytes 393232 | tf_op jit(solution)/shard_map/reduce_scatter | solution.py:115
  172.4 2.2 fusion.71
  176.8 19.5 %all-gather.8.cloned.1.call-done = bf16[1024,768]{1,0:T(8,128)(2,1)} async-done(((bf16[256,768]{1,0:T(8,128)(2,1)}), bf16[1024,768]{1,0:T(8,128)(2,1)}) %all-gather.8.cloned.1.call-update) | async-done | bytes 1572880 | tf_op jit(solution)/shard_map/all_gather | solution.py:141
  196.3 2.8 convolution_convert_fusion.3
  199.1 40.9 %while.28 = (s32[]{:T(128)}, f32[1024,3,64]{0,2,1:T(8,128)S(1)}, f32[1024,3,64]{0,2,1:T(8,128)}, f32[2,512,3,64]{1,0,3,2:T(2,128)}, s32[2]{0:T(128)S(1)}, /*inde...) while((s32[]{:T(128)}, f32[1024,3,64]{0,2,1:T(8,128)S(1)}, ...), condition=%wide.region_15.16_spmd.clone, body=%wide.region_13.15_spmd.clone.sunk | while | flops 1026587136 | bytes 54307044 | solution.py:186
  201.5 3.1 fusion.133
  204.6 2.9 multiply_reduce_fusion.8
  207.5 1.6 multiply_convert_fusion.7
  211.3 8.1 %dynamic_update_slice.19 = f32[2,512,3,64]{1,0,3,2:T(2,128)} dynamic-update-slice(f32[2,512,3,64]{1,0,3,2:T(2,128)} %get-tuple-element.380, f32[1,512,3,64]{1,0,3,2:T(1,128)S(1)} %copy.40, s32[]{:T(128)S(6)} %copy.57, s32[]{:T(128)} %constant.48.clone.1..sunk.1, s32[]{:T(128)} %constant.48.clone.1..sunk.1, s32[]{:T(128)} %constant.48.clone.1..sunk.1) | dynamic-update-slice | bytes 786436 | tf_op jit(solution)/shard_map/while/body/jit(dynamic_update_index_in_dim)/dynamic_update_slice | solution.py:96
  221.8 3.5 fusion.133
  225.2 2.9 multiply_reduce_fusion.8
  228.1 1.6 multiply_convert_fusion.7
  232.0 8.1 %dynamic_update_slice.19 = f32[2,512,3,64]{1,0,3,2:T(2,128)} dynamic-update-slice(f32[2,512,3,64]{1,0,3,2:T(2,128)} %get-tuple-element.380, f32[1,512,3,64]{1,0,3,2:T(1,128)S(1)} %copy.40, s32[]{:T(128)S(6)} %copy.57, s32[]{:T(128)} %constant.48.clone.1..sunk.1, s32[]{:T(128)} %constant.48.clone.1..sunk.1, s32[]{:T(128)} %constant.48.clone.1..sunk.1) | dynamic-update-slice | bytes 786436 | tf_op jit(solution)/shard_map/while/body/jit(dynamic_update_index_in_dim)/dynamic_update_slice | solution.py:96
  240.1 1.9 reshape.196
  243.4 1.3 maximum_convert_fusion.1
  244.7 2.6 convolution_convert_fusion
  248.4 3.1 fusion.76
  251.5 2.3 fusion.37
  253.9 1.3 fusion.75
  255.6 2.6 fusion.35
  258.9 16.7 %reduce-scatter.11.cloned.1.call-done = bf16[256,768]{1,0:T(8,128)(2,1)} async-done(((bf16[1024,768]{1,0:T(8,128)(2,1)}), bf16[256,768]{1,0:T(8,128)(2,1)}) %reduce-scatter.11.cloned.1.call-update) | async-done | bytes 393232 | tf_op jit(solution)/shard_map/reduce_scatter | solution.py:197
  275.6 1.6 multiply_reduce_fusion.3
  277.3 1.7 fusion.57
  279.0 44.5 %all-reduce.4 = (f32[768]{0:T(1024)}, f32[768]{0:T(1024)}) all-reduce(f32[768]{0:T(1024)S(1)} %get-tuple-element.138, f32[768]{0:T(1024)S(1)} %copy-done.29), channel_id=1, replica_groups=mesh['dp'=8,'tensor'=4] {'dp','tensor'}, use_global_device_ids=true, to_apply=%region_22.23 | all-reduce | flops 1536 | bytes 12288 | tf_op jit(solution)/shard_map/psum | solution.py:203
  323.5 2.4 add_add_fusion.2
  325.9 133.8 %all-reduce.8.cloned.1.call-done = (f32[768,3,192]{0,2,1:T(8,128)}, f32[192,768]{1,0:T(8,128)}, f32[768,2,288]{0,2,1:T(8,128)}, f32[288,768]{1,0:T(8,128)}) async-done(((f32[768,3,192]{0,2,1:T(8,128)}, f32[192,768]{1,0:T(8,128)}, f32[768,2,288]{0,2,1:T(8,128)}, f32[288,768]{1,0:T(8,128)}), (f32[768,3,192]{0,2,1:T(8,128)}, f32[192,768]{1,0:T(8,128)}, f32[768,2,288]{0,2,1:T(8,128)}, ...) | async-done | bytes 5013520 | tf_op jit(solution)/shard_map/psum | solution.py:204
  459.7 2.9 copy.69
  (157 shorter events, 31.5 us)
Async XLA Ops:
  7.2 2.7 copy-start
  7.2 54.1 %reduce-scatter.5.cloned.1.call-start = ((), (), s32[]{:S(2)}) async-start(), calls=%async_computation.4 | async-start | bytes 1966080 | tf_op jit(solution)/shard_map/reduce_scatter | solution.py:99
  7.3 1.9 copy-start.1
  7.3 2.6 copy-start.24
  9.2 2.0 copy-start.27
  9.9 1.4 copy-start.35
  11.2 1.4 copy-start.5
  13.9 1.9 copy-start.6
  27.3 1.2 copy-start.22
  30.3 54.1 %all-gather.4.cloned.1.call-start = ((), (), s32[]{:S(2)}) async-start(), calls=%async_computation.5 | async-start | bytes 1966080 | tf_op jit(solution)/shard_map/all_gather | solution.py:105
  33.6 30.0 %copy-start.23 = (f32[768]{0:T(1024)S(1)}, f32[768]{0:T(1024)}, u32[]{:S(2)}) copy-start(f32[768]{0:T(1024)} %param.16) | copy-start | bytes 9220
  63.4 77.9 %copy-start.26 = (f32[256]{0:T(256)}, f32[256]{0:T(256)S(1)}, u32[]{:S(2)}) copy-start(f32[256]{0:T(256)S(1)} %broadcast_multiply_fusion.4) | copy-start | bytes 3076
  63.6 25.0 %copy-start.33 = (f32[256]{0:T(256)}, f32[256]{0:T(256)S(1)}, u32[]{:S(2)}) copy-start(f32[256]{0:T(256)S(1)} %multiply_reduce_fusion.4) | copy-start | bytes 3076
  63.6 77.7 %copy-start.30 = (f32[256]{0:T(256)}, f32[256]{0:T(256)S(1)}, u32[]{:S(2)}) copy-start(f32[256]{0:T(256)S(1)} %fusion.66) | copy-start | bytes 3076
  64.6 41.2 %all-gather.6.cloned.1.call-start = ((), (), s32[]{:S(2)}) async-start(), calls=%async_computation.7 | async-start | bytes 1966080 | tf_op jit(solution)/shard_map/all_gather | solution.py:119
  65.3 76.0 %reduce-scatter.9.cloned.1.call-start = ((), (), s32[]{:S(2)}) async-start(), calls=%async_computation.8 | async-start | bytes 1966080 | tf_op jit(solution)/shard_map/reduce_scatter | solution.py:135
  105.7 4.6 copy-start.38
  109.3 0.8 copy-start.40
  109.4 1.0 copy-start.42
  113.0 59.5 %reduce-scatter.7.cloned.1.call-start = ((), (), s32[]{:S(2)}) async-start(), calls=%async_computation.6 | async-start | bytes 1966080 | tf_op jit(solution)/shard_map/reduce_scatter | solution.py:115
  113.0 3.0 copy-start.39
  115.1 0.9 copy-start.20
  118.2 78.1 %all-gather.8.cloned.1.call-start = ((), (), s32[]{:S(2)}) async-start(), calls=%async_computation.9 | async-start | bytes 1966080 | tf_op jit(solution)/shard_map/all_gather | solution.py:141
  143.2 32.3 %copy-start.8 = (bf16[256,768]{1,0:T(8,128)(2,1)S(1)}, bf16[256,768]{1,0:T(8,128)(2,1)}, u32[]{:S(2)}) copy-start(bf16[256,768]{1,0:T(8,128)(2,1)} %param.19) | copy-start | bytes 1179652
  174.7 0.9 copy-start.3
  174.7 0.9 copy-start.31
  176.5 99.2 %reduce-scatter.11.cloned.1.call-start = ((), (), s32[]{:S(2)}) async-start(), calls=%async_computation.10 | async-start | bytes 1966080 | tf_op jit(solution)/shard_map/reduce_scatter | solution.py:197
  240.1 1.9 copy-start.15
  242.1 1.0 copy-start.13
  247.3 1.1 copy-start.21
  247.3 4.1 copy-start.41
  247.4 212.4 %all-reduce.8.cloned.1.call-start = ((), (), s32[]{:S(2)}) async-start(), calls=%async_computation.11 | async-start | bytes 10027008 | tf_op jit(solution)/shard_map/psum | solution.py:204
  248.4 3.1 copy-start.37
  248.4 3.1 copy-start.43
  251.5 2.3 copy-start.11
  251.5 2.3 copy-start.17
  253.8 1.8 copy-start.2
  253.8 1.8 copy-start.25
  253.8 1.8 copy-start.28
  253.8 1.8 copy-start.36
  258.3 20.7 %copy-start.29 = (f32[768]{0:T(1024)S(1)}, f32[768]{0:T(1024)}, u32[]{:S(2)}) copy-start(f32[768]{0:T(1024)} %get-tuple-element.142) | copy-start | bytes 9220
  258.3 65.2 %copy-start.4 = (f32[256,768]{1,0:T(8,128)S(1)}, f32[256,768]{1,0:T(8,128)}, u32[]{:S(2)}) copy-start(f32[256,768]{1,0:T(8,128)} %copy-done.3) | copy-start | bytes 2359300
  258.3 65.2 %copy-start.9 = (bf16[256,768]{1,0:T(8,128)(2,1)S(1)}, bf16[256,768]{1,0:T(8,128)(2,1)}, u32[]{:S(2)}) copy-start(bf16[256,768]{1,0:T(8,128)(2,1)} %param.19) | copy-start | bytes 1179652
  258.3 65.2 %copy-start.32 = (f32[256]{0:T(256)S(1)}, f32[256]{0:T(256)}, u32[]{:S(2)}) copy-start(f32[256]{0:T(256)} %copy-done.31) | copy-start | bytes 3076
  275.6 47.9 %copy-start.7 = (bf16[256,768]{1,0:T(8,128)(2,1)S(1)}, bf16[256,768]{1,0:T(8,128)(2,1)}, u32[]{:S(2)}) copy-start(bf16[256,768]{1,0:T(8,128)(2,1)} %reduce-scatter.11.cloned.1.call-done) | copy-start | bytes 1179652
  459.7 3.0 copy-start.19
  459.7 3.8 copy-start.16
  463.5 1.8 copy-start.18
  (4 other events, 2.9 us)
Sparse Core Ops, SparseCore 0:
  30.4 30.8 reduce-scatter.4
  64.7 19.6 all-gather.3
  86.0 19.6 all-gather.5
  113.1 28.1 reduce-scatter.8
  144.2 28.1 reduce-scatter.6
  176.6 19.6 all-gather.7
  247.5 28.1 reduce-scatter.10
  280.2 179.4 all-reduce.7
where the time goes:
time: 475 us; the launch traced here: 473 us
  waiting for transfers between devices  286 us (60%)
  matrix products  54.3 us (11%)
  blocking collectives  44.5 us (9%)
  local copies, waits for them, and re-layouts  37.7 us (8%)
  other arithmetic  32.5 us (7%)
  between operations  14.7 us (3%)
    psum x1, waiting for transfers between devices, on_device(): lax.psum((grad_joint_w, grad_output, grad_expand, grad_shrink), 'dp')  134 us
    psum x1, blocking collectives, on_device(): lax.psum((gain_one_part, gain_two_part), ('dp', 'tensor'))  44.5 us
    reduce_scatter x1, waiting for transfers between devices, on_device(): lax.psum_scatter(shrink_part.astype(jnp.bfloat16), 'tensor', scatter_dime...  27.9 us
    reduce_scatter x1, waiting for transfers between devices, on_device(): lax.psum_scatter(branch_part.astype(jnp.bfloat16), 'tensor', scatter_dime...  27.7 us
    reduce_scatter x1, waiting for transfers between devices, on_device(): lax.psum_scatter(second_part.astype(jnp.bfloat16), 'tensor', scatter_dime...  23.1 us
    all_gather x1, waiting for transfers between devices, on_device(): lax.all_gather(grad_middle.astype(jnp.bfloat16), 'tensor', axis=0, tiled=...  19.5 us
    all_gather x1, waiting for transfers between devices, on_device(): second = lax.all_gather(second_own, 'tensor', axis=0, tiled=True)  18.9 us
    all_gather x1, waiting for transfers between devices, on_device(): grad_rows = lax.all_gather(cotangent, 'tensor', axis=0, tiled=True)  17.2 us
  transfers between devices with their start and end apart: 8, of which 8 were waited for; matrix products, arithmetic and copies ran while one was open for 6% of the time, Pallas kernels for 0%

commit v1 on v0

v1 whole, which is shorter than its diff:
```python
import functools

import jax
import jax.numpy as jnp
import numpy as np
from jax import lax
from jax.experimental import pallas as pl
from jax.experimental.pallas import tpu as pltpu
from jax.sharding import PartitionSpec as P

HEAD_DIM = 64
SEQ_LEN = 1024
EPS = 1e-05
THETA = 160000.0
SCALE = HEAD_DIM**-0.5
CHUNKS = 2
VMEM_LIMIT = 48 * 1024 * 1024
F32 = jnp.float32
BF16 = jnp.bfloat16
VMEM = pl.BlockSpec(memory_space=pltpu.VMEM)


def dot(a, b, dims=((1,), (0,))):
    return lax.dot_general(a, b, (dims, ((), ())), preferred_element_type=F32)


def norm_parts(values):
    centred = values - jnp.mean(values, axis=-1, keepdims=True)
    inverse = lax.rsqrt(jnp.mean(centred * centred, axis=-1, keepdims=True) + EPS)
    return centred * inverse, inverse


def norm_back(hat, inverse, gain, grad):
    scaled = grad * gain
    return inverse * (
        scaled
        - jnp.mean(scaled, axis=-1, keepdims=True)
        - hat * jnp.mean(scaled * hat, axis=-1, keepdims=True)
    )


def head_rows(array, head):
    index = lax.broadcasted_iota(jnp.int32, array.shape, 0) // HEAD_DIM
    return jnp.where(index == head, array, jnp.zeros_like(array))


def head_columns(array, head):
    index = lax.broadcasted_iota(jnp.int32, array.shape, 1) // HEAD_DIM
    return jnp.where(index == head, array, jnp.zeros_like(array))


def attend_kernel(heads, key, query_t, value_t, mixed_t, logsum):
    for head in range(heads):
        rows = slice(head * HEAD_DIM, (head + 1) * HEAD_DIM)
        scores = dot(key[...], head_rows(query_t[...], head)) * SCALE
        peak = jnp.max(scores, axis=0, keepdims=True)
        exps = jnp.exp(scores - peak)
        total = jnp.sum(exps, axis=0, keepdims=True)
        probs = (exps * (1.0 / total)).astype(BF16)
        mixed_t[rows, :] = dot(value_t[rows, :], probs).astype(BF16)
        logsum[head : head + 1, :] = peak + jnp.log(total)


def attend(key, query_t, value_t, heads, block):
    width, rows = query_t.shape
    per_seq = SEQ_LEN // block
    return pl.pallas_call(
        functools.partial(attend_kernel, heads),
        grid=(rows // block,),
        in_specs=[
            pl.BlockSpec((SEQ_LEN, width), lambda i: (i // per_seq, 0)),
            pl.BlockSpec((width, block), lambda i: (0, i)),
            pl.BlockSpec((width, SEQ_LEN), lambda i: (0, i // per_seq)),
        ],
        out_specs=[
            pl.BlockSpec((width, block), lambda i: (0, i)),
            pl.BlockSpec((8, block), lambda i: (0, i)),
        ],
        out_shape=[
            jax.ShapeDtypeStruct((width, rows), BF16),
            jax.ShapeDtypeStruct((8, rows), F32),
        ],
        compiler_params=pltpu.CompilerParams(vmem_limit_bytes=VMEM_LIMIT),
        name="attend",
    )(key, query_t, value_t)


def attend_back_kernel(
    heads, per_seq, key, key_t, query, query_t, value, grad, grad_t, logsum, dq_t, dk, dv
):
    @pl.when(pl.program_id(0) % per_seq == 0)
    def _():
        dk[...] = jnp.zeros_like(dk)
        dv[...] = jnp.zeros_like(dv)

    for head in range(heads):
        rows = slice(head * HEAD_DIM, (head + 1) * HEAD_DIM)
        scores = dot(key[...], head_rows(query_t[...], head)) * SCALE
        probs = jnp.exp(scores - logsum[head : head + 1, :])
        dprobs = dot(value[...], head_rows(grad_t[...], head))
        product = probs * dprobs
        delta = jnp.sum(product, axis=0, keepdims=True)
        dscores = (product - probs * delta).astype(BF16)
        dq_t[rows, :] = dot(key_t[rows, :], dscores) * SCALE
        dk[...] += dot(dscores, head_columns(query[...], head)) * SCALE
        dv[...] += dot(probs.astype(BF16), head_columns(grad[...], head))


def attend_back(key, key_t, query, query_t, value, grad, grad_t, logsum, heads, block):
    width, rows = query_t.shape
    per_seq = SEQ_LEN // block
    seq_down = pl.BlockSpec((SEQ_LEN, width), lambda i: (i // per_seq, 0))
    seq_across = pl.BlockSpec((width, SEQ_LEN), lambda i: (0, i // per_seq))
    down = pl.BlockSpec((block, width), lambda i: (i, 0))
    across = pl.BlockSpec((width, block), lambda i: (0, i))
    return pl.pallas_call(
        functools.partial(attend_back_kernel, heads, per_seq),
        grid=(rows // block,),
        in_specs=[
            seq_down,
            seq_across,
            down,
            across,
            seq_down,
            down,
            across,
            pl.BlockSpec((8, block), lambda i: (0, i)),
        ],
        out_specs=[across, seq_down, seq_down],
        out_shape=[
            jax.ShapeDtypeStruct((width, rows), F32),
            jax.ShapeDtypeStruct((rows, width), F32),
            jax.ShapeDtypeStruct((rows, width), F32),
        ],
        compiler_params=pltpu.CompilerParams(vmem_limit_bytes=VMEM_LIMIT),
        cost_estimate=pl.CostEstimate(
            flops=16 * rows * SEQ_LEN * width, bytes_accessed=16 * rows * width, transcendentals=0
        ),
        name="attend_back",
    )(key, key_t, query, query_t, value, grad, grad_t, logsum)


def exchange_kernel(sums, extras, gather, step, own, *refs):
    parts = refs[:sums]
    extra = refs[sums : sums + extras]
    outs = refs[sums + extras : -7]
    from_core, to_side, from_side, core_send, core_recv, side_send, side_recv = refs[-7:]
    me = lax.axis_index("tensor")
    side, core = me // 2, me % 2
    core_peer = side * 2 + (1 - core)
    side_peer = (1 - side) * 2 + core
    cross = (1 - side) * 2 + (1 - core)
    rows = own // CHUNKS

    barrier = pltpu.get_barrier_semaphore()
    for peer in (core_peer, side_peer):
        pl.semaphore_signal(
            barrier, inc=1, device_id={"tensor": peer}, device_id_type=pl.DeviceIdType.MESH
        )
    pl.semaphore_wait(barrier, 2)

    def at(owner, chunk):
        return pl.ds(pl.multiple_of(owner * own + chunk * rows, 16), rows)

    def here(chunk):
        return pl.ds(chunk * rows, rows)

    def send(src, dst, peer, slot, chunk, cores):
        copy = pltpu.make_async_remote_copy(
            src_ref=src,
            dst_ref=dst,
            send_sem=(core_send if cores else side_send).at[slot, chunk],
            recv_sem=(core_recv if cores else side_recv).at[slot, chunk],
            device_id={"tensor": peer},
            device_id_type=pl.DeviceIdType.MESH,
        )
        copy.start()
        return copy

    onward, mine, sideways = {}, {}, {}
    for slot in range(sums):
        for chunk in range(CHUNKS):
            onward[slot, chunk] = send(
                parts[slot].at[at(cross, chunk)],
                from_core.at[2 * slot, here(chunk)],
                core_peer,
                2 * slot,
                chunk,
                True,
            )
    for slot in range(sums):
        for chunk in range(CHUNKS):
            mine[slot, chunk] = send(
                parts[slot].at[at(core_peer, chunk)],
                from_core.at[2 * slot + 1, here(chunk)],
                core_peer,
                2 * slot + 1,
                chunk,
                True,
            )
    for slot in range(sums):
        for chunk in range(CHUNKS):
            onward[slot, chunk].wait_recv()
            to_side[slot, here(chunk)] = (
                parts[slot][at(side_peer, chunk)].astype(F32)
                + from_core[2 * slot, here(chunk)].astype(F32)
            ).astype(BF16)
            sideways[slot, chunk] = send(
                to_side.at[slot, here(chunk)],
                from_side.at[slot, here(chunk)],
                side_peer,
                slot,
                chunk,
                False,
            )
    sent = []
    gathered = []
    for chunk in range(CHUNKS):
        totals = []
        for slot in range(sums):
            mine[slot, chunk].wait_recv()
            sideways[slot, chunk].wait_recv()
            totals.append(
                parts[slot][at(me, chunk)].astype(F32)
                + from_core[2 * slot + 1, here(chunk)].astype(F32)
                + from_side[slot, here(chunk)].astype(F32)
            )
        result = step(chunk, at(me, chunk), here(chunk), totals, extra, outs)
        if gather:
            whole = outs[0]
            whole[at(me, chunk), :] = result
            block = whole.at[at(me, chunk)]
            over = send(block, block, side_peer, sums, chunk, False)
            near = send(block, block, core_peer, 2 * sums, chunk, True)
            gathered.append((over, near))
            sent += [over, near]
    relayed = []
    for chunk, (over, _) in enumerate(gathered):
        over.wait_recv()
        block = outs[0].at[at(side_peer, chunk)]
        relay = send(block, block, core_peer, 2 * sums + 1, chunk, True)
        relayed.append(relay)
        sent.append(relay)
    for _, near in gathered:
        near.wait_recv()
    for relay in relayed:
        relay.wait_recv()
    for copy in [*onward.values(), *mine.values(), *sideways.values(), *sent]:
        copy.wait_send()


def exchange(name, number, parts, extra, step, gather, out_shape):
    own = parts[0].shape[0] // 4
    width = parts[0].shape[1]
    sums = len(parts)
    core_slots = 2 * sums + (2 if gather else 0)
    side_slots = sums + (1 if gather else 0)
    return pl.pallas_call(
        functools.partial(exchange_kernel, sums, len(extra), gather, step, own),
        in_specs=[VMEM] * (sums + len(extra)),
        out_specs=[VMEM] * len(out_shape),
        out_shape=out_shape,
        scratch_shapes=[
            pltpu.VMEM((2 * sums, own, width), BF16),
            pltpu.VMEM((sums, own, width), BF16),
            pltpu.VMEM((sums, own, width), BF16),
            pltpu.SemaphoreType.DMA((core_slots, CHUNKS)),
            pltpu.SemaphoreType.DMA((core_slots, CHUNKS)),
            pltpu.SemaphoreType.DMA((side_slots, CHUNKS)),
            pltpu.SemaphoreType.DMA((side_slots, CHUNKS)),
        ],
        compiler_params=pltpu.CompilerParams(
            collective_id=number, has_side_effects=True, vmem_limit_bytes=VMEM_LIMIT
        ),
        name=name,
    )(*parts, *extra)


def middle_step(chunk, rows, here, totals, extra, outs):
    tokens, gain = extra
    _, middle = outs
    value = tokens[rows, :].astype(F32) + totals[0]
    middle[here, :] = value
    hat, _ = norm_parts(value)
    return (hat * gain[...]).astype(BF16)


def middle_back_step(chunk, rows, here, totals, extra, outs):
    middle, gain, cotangent = extra
    _, grad_middle, grad_gain = outs
    hat, inverse = norm_parts(middle[here, :])
    value = cotangent[here, :].astype(F32) + norm_back(hat, inverse, gain[...], totals[0])
    grad_middle[here, :] = value
    term = jnp.sum(totals[0] * hat, axis=0, keepdims=True)
    if chunk == 0:
        grad_gain[...] = term
    else:
        grad_gain[...] += term
    return value.astype(BF16)


def last_step(chunk, rows, here, totals, extra, outs):
    tokens, gain, middle, grad_middle = extra
    grad_tokens, block_out = outs
    hat, inverse = norm_parts(tokens[rows, :].astype(F32))
    grad_tokens[here, :] = grad_middle[here, :] + norm_back(hat, inverse, gain[...], totals[0])
    block_out[here, :] = (middle[here, :] + totals[1]).astype(BF16)
    return None


def group_sum_kernel(part, total, arrived, send_sem, recv_sem):
    me = lax.axis_index("tensor")
    barrier = pltpu.get_barrier_semaphore()
    for hop in range(1, 4):
        pl.semaphore_signal(
            barrier,
            inc=1,
            device_id={"tensor": (me + hop) % 4},
            device_id_type=pl.DeviceIdType.MESH,
        )
    pl.semaphore_wait(barrier, 3)
    copies = []
    for hop in range(1, 4):
        copy = pltpu.make_async_remote_copy(
            src_ref=part,
            dst_ref=arrived.at[hop - 1],
            send_sem=send_sem.at[hop - 1],
            recv_sem=recv_sem.at[hop - 1],
            device_id={"tensor": (me + hop) % 4},
            device_id_type=pl.DeviceIdType.MESH,
        )
        copy.start()
        copies.append(copy)
    for copy in copies:
        copy.wait()
    value = jnp.zeros(part.shape, F32)
    for owner in range(4):
        hop = (me - owner + 4) % 4
        term = jnp.where(hop == 0, part[...], 0.0)
        for slot in range(3):
            term = term + jnp.where(hop == slot + 1, arrived[slot], 0.0)
        value = value + term
    total[...] = value


def group_sum(part):
    return pl.pallas_call(
        group_sum_kernel,
        in_specs=[VMEM],
        out_specs=VMEM,
        out_shape=jax.ShapeDtypeStruct(part.shape, F32),
        scratch_shapes=[
            pltpu.VMEM((3,) + part.shape, F32),
            pltpu.SemaphoreType.DMA((3,)),
            pltpu.SemaphoreType.DMA((3,)),
        ],
        compiler_params=pltpu.CompilerParams(collective_id=4, has_side_effects=True),
        name="group_sum",
    )(part)


def half_turn(array):
    columns = array.reshape(array.shape[0], -1, 2, HEAD_DIM // 2)
    return np.stack([-columns[:, :, 1], columns[:, :, 0]], axis=2).reshape(array.shape)


def turn_matrix(width):
    return jnp.asarray(half_turn(np.eye(width, dtype=np.float32)), BF16)


def rotary_tables(rows, heads):
    half_width = HEAD_DIM // 2
    frequency = THETA ** (-(jnp.arange(half_width, dtype=F32) * 2.0 / HEAD_DIM))
    angles = jnp.arange(SEQ_LEN, dtype=F32)[:, None] * frequency[None, :]
    angles = jnp.tile(angles, (1, 2 * heads))
    repeat = rows // SEQ_LEN
    return jnp.tile(jnp.cos(angles), (repeat, 1)), jnp.tile(jnp.sin(angles), (repeat, 1))


def on_device(
    tokens,
    first_gain,
    joint_weight,
    output_weight,
    second_gain,
    expand_weight,
    shrink_weight,
    cotangent,
):
    local_rows, model_width = tokens.shape
    own_rows = cotangent.shape[0]
    heads = joint_weight.shape[2] // HEAD_DIM
    inner = heads * HEAD_DIM
    units = expand_weight.shape[2]
    joint_flat = joint_weight.reshape(model_width, 3 * inner)
    expand_flat = expand_weight.reshape(model_width, 2 * units)
    gain_one_row = first_gain.reshape(1, model_width)
    gain_two_row = second_gain.reshape(1, model_width)
    turn = turn_matrix(inner)

    grad_rows = lax.all_gather(cotangent, "tensor", axis=0, tiled=True)

    first_hat, _ = norm_parts(tokens.astype(F32))
    normed = (first_hat * first_gain).astype(BF16)
    turned = [dot(joint_weight[:, part], turn).astype(BF16) for part in (0, 1)]
    joint = dot(normed, jnp.concatenate([joint_flat, *turned], axis=1))
    cosine, sine = rotary_tables(local_rows, heads)
    query = (joint[:, :inner] * cosine + joint[:, 3 * inner : 4 * inner] * sine).astype(BF16)
    key = (joint[:, inner : 2 * inner] * cosine + joint[:, 4 * inner :] * sine).astype(BF16)
    value = joint[:, 2 * inner : 3 * inner].astype(BF16)
    query_t, key_t, value_t = query.T, key.T, value.T
    mixed_t, logsum = attend(key, query_t, value_t, heads, 256)
    branch_part = dot(mixed_t, output_weight, ((0,), (0,))).astype(BF16)
    second, middle = exchange(
        "middle_exchange",
        1,
        [branch_part],
        [tokens, gain_two_row],
        middle_step,
        True,
        [
            jax.ShapeDtypeStruct((local_rows, model_width), BF16),
            jax.ShapeDtypeStruct((own_rows, model_width), F32),
        ],
    )
    gate_up = dot(second, expand_flat)

    def activate(gate_part, up_part):
        return jax.nn.gelu(gate_part, approximate=True) * up_part

    hidden, activate_back = jax.vjp(activate, gate_up[:, :units], gate_up[:, units:])
    hidden = hidden.astype(BF16)
    grad_hidden = dot(grad_rows, shrink_weight, ((1,), (1,)))
    grad_gate, grad_up = activate_back(grad_hidden)
    grad_both = jnp.concatenate([grad_gate, grad_up], axis=1).astype(BF16)
    second_part = dot(grad_both, expand_flat, ((1,), (1,))).astype(BF16)
    grad_branch, grad_middle, gain_two = exchange(
        "middle_back_exchange",
        2,
        [second_part],
        [middle, gain_two_row, cotangent],
        middle_back_step,
        True,
        [
            jax.ShapeDtypeStruct((local_rows, model_width), BF16),
            jax.ShapeDtypeStruct((own_rows, model_width), F32),
            jax.ShapeDtypeStruct((1, model_width), F32),
        ],
    )
    grad_shrink = dot(hidden, grad_rows, ((0,), (0,))).astype(BF16)
    grad_expand = dot(second, grad_both, ((0,), (0,))).astype(BF16)
    grad_shrink, grad_expand = lax.psum((grad_shrink, grad_expand), "dp")

    grad_mixed = dot(grad_branch, output_weight, ((1,), (1,))).astype(BF16)
    dq_t, dk, dv = attend_back(
        key, key_t, query, query_t, value, grad_mixed, grad_mixed.T, logsum, heads, 256
    )

    def turn_back(grad):
        return grad * cosine + dot((grad * sine).astype(BF16), turn, ((1,), (1,)))

    grad_joint = jnp.concatenate([turn_back(dq_t.T), turn_back(dk), dv], axis=1).astype(BF16)
    first_part = dot(grad_joint, joint_flat, ((1,), (1,)))
    gain_one = jnp.sum(first_part * first_hat, axis=0, keepdims=True)
    grad_joint_w = dot(normed, grad_joint, ((0,), (0,))).astype(BF16)
    grad_output = dot(mixed_t, grad_branch).astype(BF16)
    gains = jnp.concatenate([gain_one, gain_two], axis=0).astype(BF16)
    grad_joint_w, grad_output, gains, grad_shrink, grad_expand = lax.optimization_barrier(
        (grad_joint_w, grad_output, gains, grad_shrink, grad_expand)
    )
    grad_joint_w, grad_output, gains = lax.psum((grad_joint_w, grad_output, gains), "dp")

    shrink_part = dot(hidden, shrink_weight).astype(BF16)
    grad_tokens, block_out = exchange(
        "last_exchange",
        3,
        [first_part.astype(BF16), shrink_part],
        [tokens, gain_one_row, middle, grad_middle],
        last_step,
        False,
        [
            jax.ShapeDtypeStruct((own_rows, model_width), F32),
            jax.ShapeDtypeStruct((own_rows, model_width), BF16),
        ],
    )
    gains = group_sum(gains.astype(F32))
    return (
        block_out,
        grad_tokens,
        gains[0],
        grad_joint_w.astype(F32).reshape(model_width, 3, inner),
        grad_output.astype(F32),
        gains[1],
        grad_expand.astype(F32).reshape(model_width, 2, units),
        grad_shrink.astype(F32),
    )


def solution(mesh):
    return jax.shard_map(
        on_device,
        mesh=mesh,
        in_specs=(
            P("dp", None),
            P(),
            P(None, None, "tensor"),
            P("tensor", None),
            P(),
            P(None, None, "tensor"),
            P("tensor", None),
            P(("dp", "tensor"), None),
        ),
        out_specs=(
            P(("dp", "tensor"), None),
            P(("dp", "tensor"), None),
            P(),
            P(None, None, "tensor"),
            P("tensor", None),
            P(),
            P(None, None, "tensor"),
            P("tensor", None),
        ),
        check_vma=False,
    )
```

time: 475 us -> 308 us (0.65)
  waiting for transfers between devices: 286 us -> 102 us
  Pallas kernels: 0 us -> 96.9 us
  matrix products: 54.3 us -> 29 us
  blocking collectives: 44.5 us -> 19.9 us
  other arithmetic: 32.5 us -> 14.8 us
  local copies, waits for them, and re-layouts: 37.7 us -> 30.4 us
    pallas_call x0 -> x6, Pallas kernels: none -> 96.9 us  [the longest x3 69.4 us: exchange(): pl.pallas_call(functools.partial(exchange_kernel, sums, len(extra), gathe...]
    reduce_scatter x4 -> x0, waiting for transfers between devices: 95.4 us -> none  [the longest x1 27.9 us: on_device(): lax.psum_scatter(shrink_part.astype(jnp.bfloat16), 'tensor', scatter_dime...]
    all_gather x2 -> x0, waiting for transfers between devices: 38.4 us -> none  [the longest x1 19.5 us: on_device(): lax.all_gather(grad_middle.astype(jnp.bfloat16), 'tensor', axis=0, tiled=...]
    psum x1 -> x2, waiting for transfers between devices: 134 us -> 101 us  [the longest x1 71.3 us: on_device(): grad_shrink, grad_expand = lax.psum((grad_shrink, grad_expand), 'dp')]
    dot_general x26 -> x16, matrix products: 54.3 us -> 29 us  [dot(): return lax.dot_general(a, b, (dims, ((), ())), preferred_element_type=F32)]
    psum x1, blocking collectives: 44.5 us -> 19.9 us  [on_device(): lax.psum((grad_joint_w, grad_output, gains), 'dp')]
    all_gather x1, waiting for transfers between devices: 17.2 us -> 0.01 us  [on_device(): grad_rows = lax.all_gather(cotangent, 'tensor', axis=0, tiled=True)]
    dynamic_update_slice x4 -> x0, local copies, waits for them, and re-layouts: 17 us -> none  [on_device(): mixed_blocks, logsum = lax.map(attend, block_ids)]
  transfers between devices with their start and end apart: 8 -> 3, of which waited for: 8 -> 2; matrix products, arithmetic and copies ran while one was open for 6% -> 11% of each run, Pallas kernels for 0% -> 20%
where the time goes in v1:
time: 308 us; the launch traced here: 307 us
  waiting for transfers between devices  102 us (33%)
  Pallas kernels  96.9 us (31%)
  local copies, waits for them, and re-layouts  30.4 us (10%)
  matrix products  29 us (9%)
  blocking collectives  19.9 us (6%)
  other arithmetic  14.8 us (5%)
  between operations  14.2 us (5%)
    psum x1, waiting for transfers between devices, on_device(): grad_shrink, grad_expand = lax.psum((grad_shrink, grad_expand), 'dp')  71.3 us
    pallas_call x3, Pallas kernels, exchange(): pl.pallas_call(functools.partial(exchange_kernel, sums, len(extra), gathe...  69.4 us
    psum x1, waiting for transfers between devices, on_device(): lax.psum((grad_joint_w, grad_output, gains), 'dp')  29.5 us
    dot_general x16, matrix products, dot(): return lax.dot_general(a, b, (dims, ((), ())), preferred_element_type=F32)  29 us
    unnamed x97, local copies, waits for them, and re-layouts  20.1 us
    psum x1, blocking collectives, on_device(): lax.psum((grad_joint_w, grad_output, gains), 'dp')  19.9 us
    pallas_call x1, Pallas kernels, attend_back(): pl.pallas_call(functools.partial(attend_back_kernel, heads, per_seq), gri...  12.3 us
    pallas_call x1, Pallas kernels, attend(): pl.pallas_call(functools.partial(attend_kernel, heads), grid=(rows // blo...  10.2 us
  transfers between devices with their start and end apart: 3, of which 2 were waited for; matrix products, arithmetic and copies ran while one was open for 11% of the time, Pallas kernels for 20%

profile of v1, /device:TPU:0, one launch (start us, length us, event | category | flops | bytes accessed | tf_op | source)
XLA Modules:
  0.0 306.9 jit_solution(9701321416348377212)
XLA Ops:
  8.7 1.8 convert_reduce_fusion
  11.7 1.9 fusion.7
  13.6 1.9 copy-done.27
  15.6 1.0 copy.35.value
  17.1 3.2 %fusion.27 = (bf16[1024,192]{0,1:T(8,128)(2,1)S(1)}, bf16[1024,192]{0,1:T(8,128)(2,1)}) fusion(f32[1024,960]{0,1:T(8,128)} %copy-done.27, f32[1024,32]{0,1:T(8,128)S(1)} %get-tuple-element.62, f32[1024,32]{0,1:T(8,128)S(1)} %get-tuple-element.61), kind=kLoop, calls=%fused_computation.56 | loop fusion | flops 1572864 | bytes 4194304 | tf_op jit(solution)/shard_map/convert_element_type | solution.py:408
  20.3 1.2 copy.29.key
  21.5 1.0 copy.30.query
  22.6 1.2 slice_bitcast_fusion.value_t
  23.8 10.2 %attend.1 = (bf16[192,1024]{1,0:T(8,128)(2,1)S(1)}, f32[8,1024]{1,0:T(8,128)S(1)}) custom-call(bf16[1024,192]{1,0:T(8,128)(2,1)S(1)} %copy.29.key, bf16[192,1024]{1,0:T(8,128)(2,1)S(1)} %bitcast.75, bf16[192,1024]{1,0:T(8,128)(2,1)S(1)} %slice_bitcast_fusion.value_t), custom_call_target="tpu_custom_call" | custom-call | tf_op jit(solution)/shard_map/attend/pallas_call | solution.py:67
  35.4 23.5 %middle_exchange.1 = (bf16[1024,768]{1,0:T(8,128)(2,1)S(1)}, f32[256,768]{1,0:T(8,128)S(1)}) custom-call(bf16[1024,768]{1,0:T(8,128)(2,1)S(1)} %convolution_convert_fusion.2.refs_0_, bf16[1024,768]{1,0:T(8,128)(2,1)S(1)} %copy-done.1, f32[1,768]{1,0:T(1,128)S(1)} %reshape.83.refs_2_), custom_call_target="tpu_custom_call" | custom-call | tf_op jit(solution)/shard_map/middle_exchange/pallas_call | solution.py:258
  59.8 1.1 copy-done.25
  61.0 2.5 fusion.44
  63.5 4.5 %fusion.21 = (bf16[1024,288]{0,1:T(8,128)(2,1)S(1)}, bf16[1024,288]{0,1:T(8,128)(2,1)S(1)}, bf16[1024,288]{0,1:T(8,128)(2,1)}) fusion(f32[1024,576]{0,1:T(8,128)} %fusion.44, bf16[1024,768]{1,0:T(8,128)(2,1)} %all-gather.2.cloned.1.call-done, bf16[288,768]{1,0:T(8,128)(2,1)} %param.15), kind=kOutput, calls=%fused_computation.45 | convolution fusion | flops 460652544 | bytes 6144000 | tf_op jit(solution)/shard_map/dot_general | solution.py:24
  68.0 2.0 convolution_convert_fusion.3
  70.0 1.4 convolution_convert_fusion.refs_0_
  71.5 22.5 %middle_back_exchange.1 = (bf16[1024,768]{1,0:T(8,128)(2,1)S(1)}, f32[256,768]{1,0:T(8,128)S(1)}, f32[1,768]{1,0:T(1,128)S(1)}) custom-call(bf16[1024,768]{1,0:T(8,128)(2,1)S(1)} %convolution_convert_fusion.refs_0_, f32[256,768]{1,0:T(8,128)S(1)} %copy-done.3, f32[1,768]{1,0:T(1,128)S(1)} %reshape.83.refs_2_, bf16[256,768]{1,0:T(8,128)(2,1)S(1)} %copy-done.9), custom_call_target="tpu_custom_call" | custom-call | tf_op jit(solution)/shard_map/middle_back_exchange/pallas_call | solution.py:258
  95.0 1.1 copy-done.6
  96.1 1.4 convolution_convert_fusion.6
  97.5 2.0 copy.31.grad
  99.5 1.0 copy-done.5
  100.5 1.0 copy-done.21
  101.5 1.0 copy-done.22
  102.6 1.0 copy-done.23
  103.6 1.0 copy-done.24
  104.6 12.3 %attend_back.1 = (f32[192,1024]{1,0:T(8,128)S(1)}, f32[1024,192]{1,0:T(8,128)S(1)}, f32[1024,192]{1,0:T(8,128)S(1)}) custom-call(bf16[1024,192]{1,0:T(8,128)(2,1)S(1)} %copy.29.key, bf16[192,1024]{1,0:T(8,128)(2,1)S(1)} %bitcast.77, bf16[1024,192]{1,0:T(8,128)(2,1)S(1)} %copy-done.22, bf16[192,1024]{1,0:T(8,128)(2,1)S(1)} %bitcast.76, ...), custom_call_target="tpu_custom_call" | custom-call | flops 3221225472 | bytes 3145728 | tf_op jit(solution)/shard_map/attend_back/pallas_call | solution.py:116
  116.9 1.0 copy-done.12
  117.9 1.0 copy-done.13
  118.9 0.9 copy-done.17
  119.8 2.5 copy.32
  122.3 2.8 convolution_convert_fusion.5
  125.2 1.0 copy-done.18
  126.2 1.4 fusion.29
  127.7 1.0 fusion.14
  128.7 1.0 fusion.13
  129.7 0.9 copy.34
  130.6 4.7 %fusion.5 = (bf16[768]{0:T(1024)(128)(2,1)S(1)}, bf16[1024,768]{1,0:T(8,128)(2,1)}) fusion(bf16[1024,768]{1,0:T(8,128)(2,1)S(1)} %copy-done.1, f32[1024]{0:T(1024)S(1)} %copy-done.43, f32[1024]{0:T(1024)S(1)} %broadcast_multiply_fusion, bf16[768,576]{0,1:T(8,128)(2,1)} %bitcast.81, bf16[1024,192]{0,1:T(8,128)(2,1)} %copy.34, bf16[1024,192]{0,1:T(8,128)(2,1)} %fusion.14, ...), kind=kOutput, calls=%fused_computation.7 | convolution fusion | flops 914226432 | bytes 5219840 | tf_op jit(solution)/shard_map/dot_general | solution.py:24
  135.4 1.2 convolution_convert_fusion.7
  136.6 2.2 convolution_convert_fusion.4
  138.8 71.3 %all-reduce.7.cloned.1.call-done = (bf16[288,768]{1,0:T(8,128)(2,1)}, bf16[768,576]{0,1:T(8,128)(2,1)}) async-done(((bf16[288,768]{1,0:T(8,128)(2,1)}, bf16[768,576]{0,1:T(8,128)(2,1)}), (bf16[288,768]{1,0:T(8,128)(2,1)}, bf16[768,576]{0,1:T(8,128)(2,1)})) %all-reduce.7.cloned.1.call-update) | async-done | bytes 1327120 | tf_op jit(solution)/shard_map/psum | solution.py:452
  210.3 1.0 convolution_convert_fusion.1.refs_1_
  212.1 23.4 %last_exchange.1 = (f32[256,768]{1,0:T(8,128)S(1)}, bf16[256,768]{1,0:T(8,128)(2,1)S(1)}) custom-call(bf16[1024,768]{1,0:T(8,128)(2,1)S(1)} %copy-done.8, bf16[1024,768]{1,0:T(8,128)(2,1)S(1)} %convolution_convert_fusion.1.refs_1_, bf16[1024,768]{1,0:T(8,128)(2,1)} %refs_2_.1, f32[1,768]{1,0:T(1,128)S(1)} %broadcast_in_dim.5.refs_3_, ...), custom_call_target="tpu_custom_call" | custom-call | tf_op jit(solution)/shard_map/last_exchange/pallas_call | solution.py:258
  236.4 19.9 %psum.37 = bf16[2,768]{1,0:T(2,128)(2,1)S(1)} all-reduce(bf16[2,768]{1,0:T(2,128)(2,1)S(1)} %pad_maximum_fusion.6), channel_id=1, replica_groups=mesh['dp'=8,'tensor'=4] {'dp'}, use_global_device_ids=true, to_apply=%region_5.0 | all-reduce | flops 1536 | bytes 6144 | tf_op jit(solution)/shard_map/psum | solution.py:471
  256.8 5.0 %group_sum.1 = f32[2,768]{1,0:T(2,128)} custom-call(f32[2,768]{1,0:T(2,128)} %convert_element_type.90.part), custom_call_target="tpu_custom_call" | custom-call | tf_op jit(solution)/shard_map/group_sum/pallas_call | solution.py:347
  261.8 1.0 convert_element_type.92
  262.8 1.3 convert.35
  264.8 29.5 %all-reduce.5.cloned.1.call-done = (bf16[768,3,192]{0,2,1:T(8,128)(2,1)}, bf16[192,768]{1,0:T(8,128)(2,1)}) async-done(((bf16[768,3,192]{0,2,1:T(8,128)(2,1)}, bf16[192,768]{1,0:T(8,128)(2,1)}), (bf16[768,3,192]{0,2,1:T(8,128)(2,1)}, bf16[192,768]{1,0:T(8,128)(2,1)})) %all-reduce.5.cloned.1.call-update) | async-done | bytes 1179664 | tf_op jit(solution)/shard_map/psum | solution.py:471
  294.3 1.8 convert_element_type.91
  296.1 2.6 reshape.86
  (107 shorter events, 11.1 us)
Async XLA Ops:
  7.2 52.6 %copy-start = (bf16[768,2,288]{0,2,1:T(8,128)(2,1)S(1)}, bf16[768,2,288]{0,2,1:T(8,128)(2,1)}, u32[]{:S(2)}) copy-start(bf16[768,2,288]{0,2,1:T(8,128)(2,1)} %param.14) | copy-start | bytes 2654212
  7.2 3.3 %copy-start.1 = (bf16[1024,768]{1,0:T(8,128)(2,1)S(1)}, bf16[1024,768]{1,0:T(8,128)(2,1)}, u32[]{:S(2)}) copy-start(bf16[1024,768]{1,0:T(8,128)(2,1)} %refs_2_.1) | copy-start | bytes 4718596
  7.2 56.3 %all-gather.2.cloned.1.call-start = ((), (), s32[]{:S(2)}) async-start(), calls=%async_computation | async-start | bytes 1966080 | tf_op jit(solution)/shard_map/all_gather | solution.py:401
  7.9 202.2 %all-reduce.7.cloned.1.call-start = ((), (), s32[]{:S(2)}) async-start(), calls=%async_computation.2 | async-start | bytes 2654208 | tf_op jit(solution)/shard_map/psum | solution.py:452
  8.7 2.4 copy-start.28
  8.7 2.4 copy-start.37
  10.4 1.3 copy-start.41
  13.6 1.9 copy-start.27
  17.1 3.2 %copy-start.30 = (f32[1024,32]{0,1:T(8,128)}, f32[1024,32]{0,1:T(8,128)S(1)}, u32[]{:S(2)}) copy-start(f32[1024,32]{0,1:T(8,128)S(1)} %get-tuple-element.62) | copy-start | bytes 393220
  22.5 12.2 %copy-start.38 = (bf16[192,768]{1,0:T(8,128)(2,1)S(1)}, bf16[192,768]{1,0:T(8,128)(2,1)}, u32[]{:S(2)}) copy-start(bf16[192,768]{1,0:T(8,128)(2,1)} %param.12) | copy-start | bytes 884740
  58.9 0.9 copy-start.2
  59.8 1.1 copy-start.25
  63.5 4.5 %copy-start.26 = (bf16[1024,768]{1,0:T(8,128)(2,1)S(1)}, bf16[1024,768]{1,0:T(8,128)(2,1)}, u32[]{:S(2)}) copy-start(bf16[1024,768]{1,0:T(8,128)(2,1)} %copy-done.25) | copy-start | bytes 4718596
  70.0 1.5 copy-start.3
  70.0 1.5 copy-start.9
  71.5 24.6 %copy-start.39 = (bf16[192,768]{1,0:T(8,128)(2,1)S(1)}, bf16[192,768]{1,0:T(8,128)(2,1)}, u32[]{:S(2)}) copy-start(bf16[192,768]{1,0:T(8,128)(2,1)} %param.12) | copy-start | bytes 884740
  94.1 0.9 copy-start.15
  95.0 1.1 copy-start.6
  99.5 1.0 copy-start.5
  100.5 1.0 copy-start.21
  101.5 1.0 copy-start.22
  102.6 1.0 copy-start.23
  103.6 1.0 copy-start.24
  116.9 1.0 copy-start.12
  117.9 1.0 copy-start.13
  118.9 0.9 copy-start.17
  119.8 2.5 copy-start.45
  122.3 2.9 copy-start.31
  125.1 1.1 copy-start.18
  125.1 169.2 %all-reduce.5.cloned.1.call-start = ((), (), s32[]{:S(2)}) async-start(), calls=%async_computation.1 | async-start | bytes 2359296 | tf_op jit(solution)/shard_map/psum | solution.py:471
  126.2 1.4 copy-start.29
  127.7 2.1 copy-start.14
  128.7 2.0 copy-start.43
  130.6 4.7 %copy-start.7 = (bf16[1024,768]{1,0:T(8,128)(2,1)S(1)}, bf16[1024,768]{1,0:T(8,128)(2,1)}, u32[]{:S(2)}) copy-start(bf16[1024,768]{1,0:T(8,128)(2,1)} %copy-done.6) | copy-start | bytes 4718596
  130.6 4.7 %copy-start.11 = (bf16[192,1024]{1,0:T(8,128)(2,1)S(1)}, bf16[192,1024]{1,0:T(8,128)(2,1)}, u32[]{:S(2)}) copy-start(bf16[192,1024]{1,0:T(8,128)(2,1)} %copy-done.10) | copy-start | bytes 1179652
  135.3 1.3 copy-start.34
  135.3 1.3 copy-start.35
  135.3 1.3 copy-start.36
  136.6 73.6 %copy-start.44 = (bf16[288,768]{1,0:T(8,128)(2,1)S(1)}, bf16[288,768]{1,0:T(8,128)(2,1)}, u32[]{:S(2)}) copy-start(bf16[288,768]{1,0:T(8,128)(2,1)} %param.15) | copy-start | bytes 1327108
  136.6 73.7 %copy-start.46 = (bf16[1024,288]{0,1:T(8,128)(2,1)S(1)}, bf16[1024,288]{0,1:T(8,128)(2,1)}, u32[]{:S(2)}) copy-start(bf16[1024,288]{0,1:T(8,128)(2,1)} %get-tuple-element.54) | copy-start | bytes 1769476
  210.2 1.1 copy-start.16
  210.2 1.4 copy-start.4
  210.2 1.9 copy-start.8
  212.1 49.8 %copy-start.33 = (bf16[288,768]{1,0:T(8,128)(2,1)S(1)}, bf16[288,768]{1,0:T(8,128)(2,1)}, u32[]{:S(2)}) copy-start(bf16[288,768]{1,0:T(8,128)(2,1)} %get-tuple-element.41) | copy-start | bytes 1327108
  235.5 0.9 copy-start.19
  236.3 26.5 %copy-start.32 = (bf16[768,576]{0,1:T(8,128)(2,1)S(1)}, bf16[768,576]{0,1:T(8,128)(2,1)}, u32[]{:S(2)}) copy-start(bf16[768,576]{0,1:T(8,128)(2,1)} %get-tuple-element.40) | copy-start | bytes 2654212
  262.8 1.3 copy-start.40
  296.1 3.3 %copy-start.20 = (f32[256,768]{1,0:T(8,128)S(1)}, f32[256,768]{1,0:T(8,128)}, u32[]{:S(2)}) copy-start(f32[256,768]{1,0:T(8,128)} %copy-done.19) | copy-start | bytes 2359300
  (2 other events, 1.3 us)
Sparse Core Ops, SparseCore 0:
  9.6 22.3 all-gather.1
  125.2 84.8 all-reduce.6
  214.7 79.5 all-reduce.4

commit v2 on v1

v2 whole, which is shorter than its diff:
```python
import functools

import jax
import jax.numpy as jnp
import numpy as np
from jax import lax
from jax.experimental import pallas as pl
from jax.experimental.pallas import tpu as pltpu
from jax.sharding import PartitionSpec as P

HEAD_DIM = 64
SEQ_LEN = 1024
EPS = 1e-05
THETA = 160000.0
SCALE = HEAD_DIM**-0.5
CHUNKS = 2
WAVES = 2
VMEM_LIMIT = 48 * 1024 * 1024
F32 = jnp.float32
BF16 = jnp.bfloat16
VMEM = pl.BlockSpec(memory_space=pltpu.VMEM)


def dot(a, b, dims=((1,), (0,))):
    return lax.dot_general(a, b, (dims, ((), ())), preferred_element_type=F32)


def norm_parts(values):
    centred = values - jnp.mean(values, axis=-1, keepdims=True)
    inverse = lax.rsqrt(jnp.mean(centred * centred, axis=-1, keepdims=True) + EPS)
    return centred * inverse, inverse


def norm_back(hat, inverse, gain, grad):
    scaled = grad * gain
    return inverse * (
        scaled
        - jnp.mean(scaled, axis=-1, keepdims=True)
        - hat * jnp.mean(scaled * hat, axis=-1, keepdims=True)
    )


def head_rows(array, head):
    index = lax.broadcasted_iota(jnp.int32, array.shape, 0) // HEAD_DIM
    return jnp.where(index == head, array, jnp.zeros_like(array))


def head_columns(array, head):
    index = lax.broadcasted_iota(jnp.int32, array.shape, 1) // HEAD_DIM
    return jnp.where(index == head, array, jnp.zeros_like(array))


def attend_kernel(heads, key, query_t, value_t, mixed_t, logsum):
    for head in range(heads):
        rows = slice(head * HEAD_DIM, (head + 1) * HEAD_DIM)
        scores = dot(key[...], head_rows(query_t[...], head))
        peak = jnp.max(scores, axis=0, keepdims=True)
        exps = jnp.exp(scores - peak)
        total = jnp.sum(exps, axis=0, keepdims=True)
        mixed_t[rows, :] = (dot(value_t[rows, :], exps.astype(BF16)) * (1.0 / total)).astype(BF16)
        logsum[head : head + 1, :] = peak + jnp.log(total)


def attend(key, query_t, value_t, heads, block):
    width, rows = query_t.shape
    per_seq = SEQ_LEN // block
    return pl.pallas_call(
        functools.partial(attend_kernel, heads),
        grid=(rows // block,),
        in_specs=[
            pl.BlockSpec((SEQ_LEN, width), lambda i: (i // per_seq, 0)),
            pl.BlockSpec((width, block), lambda i: (0, i)),
            pl.BlockSpec((width, SEQ_LEN), lambda i: (0, i // per_seq)),
        ],
        out_specs=[
            pl.BlockSpec((width, block), lambda i: (0, i)),
            pl.BlockSpec((8, block), lambda i: (0, i)),
        ],
        out_shape=[
            jax.ShapeDtypeStruct((width, rows), BF16),
            jax.ShapeDtypeStruct((8, rows), F32),
        ],
        compiler_params=pltpu.CompilerParams(vmem_limit_bytes=VMEM_LIMIT),
        name="attend",
    )(key, query_t, value_t)


def attend_back_kernel(
    heads, per_seq, key, key_t, query, query_t, value, grad, grad_t, mixed_t, logsum, dq_t, dk, dv
):
    @pl.when(pl.program_id(0) % per_seq == 0)
    def _():
        dk[...] = jnp.zeros_like(dk)
        dv[...] = jnp.zeros_like(dv)

    for head in range(heads):
        rows = slice(head * HEAD_DIM, (head + 1) * HEAD_DIM)
        scores = dot(key[...], head_rows(query_t[...], head))
        probs = jnp.exp(scores - logsum[head : head + 1, :])
        dprobs = dot(value[...], head_rows(grad_t[...], head))
        delta = jnp.sum(
            grad_t[rows, :].astype(F32) * mixed_t[rows, :].astype(F32), axis=0, keepdims=True
        )
        dscores = (probs * (dprobs - delta)).astype(BF16)
        dq_t[rows, :] = dot(key_t[rows, :], dscores) * SCALE
        dk[...] += dot(dscores, head_columns(query[...], head))
        dv[...] += dot(probs.astype(BF16), head_columns(grad[...], head))


def attend_back(key, key_t, query, query_t, value, grad, grad_t, mixed_t, logsum, heads, block):
    width, rows = query_t.shape
    per_seq = SEQ_LEN // block
    seq_down = pl.BlockSpec((SEQ_LEN, width), lambda i: (i // per_seq, 0))
    seq_across = pl.BlockSpec((width, SEQ_LEN), lambda i: (0, i // per_seq))
    down = pl.BlockSpec((block, width), lambda i: (i, 0))
    across = pl.BlockSpec((width, block), lambda i: (0, i))
    return pl.pallas_call(
        functools.partial(attend_back_kernel, heads, per_seq),
        grid=(rows // block,),
        in_specs=[
            seq_down,
            seq_across,
            down,
            across,
            seq_down,
            down,
            across,
            across,
            pl.BlockSpec((8, block), lambda i: (0, i)),
        ],
        out_specs=[across, seq_down, seq_down],
        out_shape=[
            jax.ShapeDtypeStruct((width, rows), F32),
            jax.ShapeDtypeStruct((rows, width), F32),
            jax.ShapeDtypeStruct((rows, width), F32),
        ],
        compiler_params=pltpu.CompilerParams(vmem_limit_bytes=VMEM_LIMIT),
        cost_estimate=pl.CostEstimate(
            flops=16 * rows * SEQ_LEN * width, bytes_accessed=16 * rows * width, transcendentals=0
        ),
        name="attend_back",
    )(key, key_t, query, query_t, value, grad, grad_t, mixed_t, logsum)


def remote(src, dst, send_sem, recv_sem, target):
    copy = pltpu.make_async_remote_copy(
        src_ref=src,
        dst_ref=dst,
        send_sem=send_sem,
        recv_sem=recv_sem,
        device_id=target,
        device_id_type=pl.DeviceIdType.MESH,
    )
    copy.start()
    return copy


def greet(targets):
    barrier = pltpu.get_barrier_semaphore()
    for target in targets:
        pl.semaphore_signal(
            barrier, inc=1, device_id=target, device_id_type=pl.DeviceIdType.MESH
        )
    pl.semaphore_wait(barrier, len(targets))


class GroupSum:
    def __init__(self, parts, own, gather, scratch):
        self.parts, self.own, self.gather = parts, own, gather
        self.from_core, self.to_side, self.from_side = scratch[:3]
        self.core_send, self.core_recv, self.side_send, self.side_recv = scratch[3:]
        me = lax.axis_index("tensor")
        side, core = me // 2, me % 2
        self.me = me
        self.core_peer = side * 2 + (1 - core)
        self.side_peer = (1 - side) * 2 + core
        self.cross = (1 - side) * 2 + (1 - core)
        self.rows = own // CHUNKS
        self.unsent = []

    def peers(self):
        return [{"tensor": self.core_peer}, {"tensor": self.side_peer}]

    def at(self, owner, chunk):
        return pl.ds(pl.multiple_of(owner * self.own + chunk * self.rows, 16), self.rows)

    def here(self, chunk):
        return pl.ds(chunk * self.rows, self.rows)

    def to_core(self, src, dst, slot, chunk):
        sems = self.core_send.at[slot, chunk], self.core_recv.at[slot, chunk]
        copy = remote(src, dst, *sems, {"tensor": self.core_peer})
        self.unsent.append(copy)
        return copy

    def over(self, src, dst, slot, chunk):
        sems = self.side_send.at[slot, chunk], self.side_recv.at[slot, chunk]
        copy = remote(src, dst, *sems, {"tensor": self.side_peer})
        self.unsent.append(copy)
        return copy

    def start(self):
        self.onward, self.mine, self.sideways = {}, {}, {}
        for first, kept, owner in ((0, self.onward, self.cross), (1, self.mine, self.core_peer)):
            for slot, part in enumerate(self.parts):
                for chunk in range(CHUNKS):
                    kept[slot, chunk] = self.to_core(
                        part.at[self.at(owner, chunk)],
                        self.from_core.at[2 * slot + first, self.here(chunk)],
                        2 * slot + first,
                        chunk,
                    )

    def cross_over(self):
        for slot, part in enumerate(self.parts):
            for chunk in range(CHUNKS):
                here = self.here(chunk)
                self.onward[slot, chunk].wait_recv()
                self.to_side[slot, here] = (
                    part[self.at(self.side_peer, chunk)].astype(F32)
                    + self.from_core[2 * slot, here].astype(F32)
                ).astype(BF16)
                self.sideways[slot, chunk] = self.over(
                    self.to_side.at[slot, here], self.from_side.at[slot, here], slot, chunk
                )

    def total(self, slot, chunk):
        here = self.here(chunk)
        self.mine[slot, chunk].wait_recv()
        self.sideways[slot, chunk].wait_recv()
        return (
            self.parts[slot][self.at(self.me, chunk)].astype(F32)
            + self.from_core[2 * slot + 1, here].astype(F32)
            + self.from_side[slot, here].astype(F32)
        )

    def finish(self, step, extra, outs):
        sums = len(self.parts)
        gathered = []
        for chunk in range(CHUNKS):
            totals = [self.total(slot, chunk) for slot in range(sums)]
            result = step(chunk, self.at(self.me, chunk), self.here(chunk), totals, extra, outs)
            if self.gather:
                outs[0][self.at(self.me, chunk), :] = result
                block = outs[0].at[self.at(self.me, chunk)]
                over = self.over(block, block, sums, chunk)
                gathered.append((over, self.to_core(block, block, 2 * sums, chunk)))
        relayed = []
        for chunk, (over, _) in enumerate(gathered):
            over.wait_recv()
            block = outs[0].at[self.at(self.side_peer, chunk)]
            relayed.append(self.to_core(block, block, 2 * sums + 1, chunk))
        for _, near in gathered:
            near.wait_recv()
        for relay in relayed:
            relay.wait_recv()

    def close(self):
        for copy in self.unsent:
            copy.wait_send()


def exchange_kernel(sums, extras, step, own, *refs):
    work = GroupSum(refs[:sums], own, True, refs[-7:])
    greet(work.peers())
    work.start()
    work.cross_over()
    work.finish(step, refs[sums : sums + extras], refs[sums + extras : -7])
    work.close()


def exchange_scratch(sums, own, width, gather):
    core_slots = 2 * sums + (2 if gather else 0)
    side_slots = sums + (1 if gather else 0)
    return [
        pltpu.VMEM((2 * sums, own, width), BF16),
        pltpu.VMEM((sums, own, width), BF16),
        pltpu.VMEM((sums, own, width), BF16),
        pltpu.SemaphoreType.DMA((core_slots, CHUNKS)),
        pltpu.SemaphoreType.DMA((core_slots, CHUNKS)),
        pltpu.SemaphoreType.DMA((side_slots, CHUNKS)),
        pltpu.SemaphoreType.DMA((side_slots, CHUNKS)),
    ]


def exchange(name, number, parts, extra, step, out_shape):
    own = parts[0].shape[0] // 4
    sums = len(parts)
    return pl.pallas_call(
        functools.partial(exchange_kernel, sums, len(extra), step, own),
        in_specs=[VMEM] * (sums + len(extra)),
        out_specs=[VMEM] * len(out_shape),
        out_shape=out_shape,
        scratch_shapes=exchange_scratch(sums, own, parts[0].shape[1], True),
        compiler_params=pltpu.CompilerParams(
            collective_id=number, has_side_effects=True, vmem_limit_bytes=VMEM_LIMIT
        ),
        name=name,
    )(*parts, *extra)


def middle_step(chunk, rows, here, totals, extra, outs):
    tokens, gain = extra
    _, middle = outs
    value = tokens[rows, :].astype(F32) + totals[0]
    middle[here, :] = value
    hat, _ = norm_parts(value)
    return (hat * gain[...]).astype(BF16)


def middle_back_step(chunk, rows, here, totals, extra, outs):
    middle, gain, cotangent = extra
    _, grad_middle, grad_gain = outs
    hat, inverse = norm_parts(middle[here, :])
    value = cotangent[here, :].astype(F32) + norm_back(hat, inverse, gain[...], totals[0])
    grad_middle[here, :] = value
    term = jnp.sum(totals[0] * hat, axis=0, keepdims=True)
    if chunk == 0:
        grad_gain[...] = term
    else:
        grad_gain[...] += term
    return value.astype(BF16)


def last_step(chunk, rows, here, totals, extra, outs):
    tokens, gain, middle, grad_middle = extra
    grad_tokens, block_out = outs
    hat, inverse = norm_parts(tokens[rows, :].astype(F32))
    grad_tokens[here, :] = grad_middle[here, :] + norm_back(hat, inverse, gain[...], totals[0])
    block_out[here, :] = (middle[here, :] + totals[1]).astype(BF16)
    return None


class DataSum:
    def __init__(self, payload, total, scratch):
        self.payload, self.result = payload, total
        self.from_pair, self.summed, self.arrived = scratch[:3]
        self.pair_send, self.pair_recv, self.far_send, self.far_recv = scratch[3:]
        self.waves, _, self.count = payload.shape[:3]
        data = lax.axis_index("dp")
        self.outer, self.inner = data // 2, data % 2
        self.unsent = []

    def pair(self):
        return {"dp": self.outer * 2 + (1 - self.inner)}

    def far(self, hop):
        return {"dp": (self.outer + hop) % self.count * 2 + self.inner}

    def peers(self):
        return [self.pair()] + [self.far(hop) for hop in range(1, self.count)]

    def place(self, hop):
        return (self.outer + hop) % self.count

    def behind(self, hop):
        return (self.outer + self.count - hop) % self.count

    def to_pair(self, src, dst, *sem):
        copy = remote(src, dst, self.pair_send.at[sem], self.pair_recv.at[sem], self.pair())
        self.unsent.append(copy)
        return copy

    def to_far(self, src, dst, hop, *sem):
        copy = remote(src, dst, self.far_send.at[sem], self.far_recv.at[sem], self.far(hop))
        self.unsent.append(copy)
        return copy

    def hops(self):
        return [*range(1, self.count), 0]

    def start(self):
        self.near = {
            (wave, hop): self.to_pair(
                self.payload.at[wave, 1 - self.inner, self.place(hop)],
                self.from_pair.at[wave, hop],
                0,
                wave,
                hop,
            )
            for wave in range(self.waves)
            for hop in self.hops()
        }
        self.spread = {}
        self.shared = {}

    def scatter(self, wave):
        for hop in self.hops():
            self.near[wave, hop].wait_recv()
            self.summed[wave, hop] = (
                self.payload[wave, self.inner, self.place(hop)].astype(F32)
                + self.from_pair[wave, hop].astype(F32)
            ).astype(BF16)
            if hop:
                self.spread[wave, hop] = self.to_far(
                    self.summed.at[wave, hop], self.arrived.at[wave, hop - 1], hop, 0, wave, hop
                )

    def collect(self, wave):
        value = self.summed[wave, 0].astype(F32)
        for hop in range(1, self.count):
            self.spread[wave, hop].wait_recv()
            value = value + self.arrived[wave, hop - 1].astype(F32)
        self.result[wave, self.inner, self.outer] = value.astype(BF16)
        block = self.result.at[wave, self.inner, self.outer]
        for hop in range(1, self.count):
            self.shared[wave, hop] = self.to_far(block, block, hop, 1, wave, hop)
        self.shared[wave, 0] = self.to_pair(block, block, 1, wave, 0)

    def relay(self, wave):
        for hop in range(1, self.count):
            self.shared[wave, hop].wait_recv()
            block = self.result.at[wave, self.inner, self.behind(hop)]
            self.near[wave, hop] = self.to_pair(block, block, 1, wave, hop)

    def finish(self):
        for wave in range(self.waves):
            self.shared[wave, 0].wait_recv()
            for hop in range(1, self.count):
                self.near[wave, hop].wait_recv()

    def close(self):
        for copy in self.unsent:
            copy.wait_send()


class GainSum:
    def __init__(self, terms, total, group, data, scratch):
        self.terms, self.total, self.group, self.data = terms, total, group, data
        self.held, self.paired, self.outer = scratch[:3]
        self.send, self.recv = scratch[3:]
        self.unsent = []

    def copy(self, src, dst, target, sem):
        copy = remote(src, dst, self.send.at[sem], self.recv.at[sem], target)
        self.unsent.append(copy)
        return copy

    def start(self):
        me = self.group.me
        self.held[me] = self.terms[...]
        self.first = [
            self.copy(self.held.at[me], self.held.at[me], {"tensor": (me + hop) % 4}, hop - 1)
            for hop in range(1, 4)
        ]

    def pair_up(self):
        for copy in self.first:
            copy.wait_recv()
        self.paired[0] = (self.held[0] + self.held[1]) + (self.held[2] + self.held[3])
        self.second = self.copy(self.paired.at[0], self.paired.at[1], self.data.pair(), 3)

    def spread(self):
        self.second.wait_recv()
        outer = self.data.outer
        self.outer[outer] = self.paired[0] + self.paired[1]
        self.third = [
            self.copy(self.outer.at[outer], self.outer.at[outer], self.data.far(hop), 3 + hop)
            for hop in range(1, self.data.count)
        ]

    def finish(self):
        for copy in self.third:
            copy.wait_recv()
        value = self.outer[0]
        for number in range(1, self.data.count):
            value = value + self.outer[number]
        self.total[...] = value

    def close(self):
        for copy in self.unsent:
            copy.wait_send()


def last_kernel(own, *refs):
    first_part, shrink_part, payload, terms, *extra = refs[:8]
    grad_tokens, block_out, summed, gains = refs[8:12]
    scratch = refs[12:]
    group = GroupSum((first_part, shrink_part), own, False, scratch[:7])
    data = DataSum(payload, summed, scratch[7:14])
    gain = GainSum(terms, gains, group, data, scratch[14:])
    greet(group.peers() + [{"tensor": group.cross}] + data.peers())
    data.start()
    gain.start()
    group.start()
    group.cross_over()
    gain.pair_up()
    for wave in range(data.waves):
        data.scatter(wave)
        if wave:
            data.collect(wave - 1)
    data.collect(data.waves - 1)
    gain.spread()
    group.finish(last_step, extra, (grad_tokens, block_out))
    for wave in range(data.waves):
        data.relay(wave)
    gain.finish()
    data.finish()
    for work in (group, data, gain):
        work.close()


def last_exchange(first_part, shrink_part, payload, terms, *extra):
    own, width = first_part.shape[0] // 4, first_part.shape[1]
    waves, _, count, rows, _ = payload.shape
    pieces = (waves, count, rows, width)
    return pl.pallas_call(
        functools.partial(last_kernel, own),
        in_specs=[VMEM] * 8,
        out_specs=[VMEM] * 4,
        out_shape=[
            jax.ShapeDtypeStruct((own, width), F32),
            jax.ShapeDtypeStruct((own, width), BF16),
            jax.ShapeDtypeStruct(payload.shape, BF16),
            jax.ShapeDtypeStruct(terms.shape, F32),
        ],
        scratch_shapes=[
            *exchange_scratch(2, own, width, False),
            pltpu.VMEM(pieces, BF16),
            pltpu.VMEM(pieces, BF16),
            pltpu.VMEM(pieces, BF16),
            pltpu.SemaphoreType.DMA((2, waves, count)),
            pltpu.SemaphoreType.DMA((2, waves, count)),
            pltpu.SemaphoreType.DMA((2, waves, count)),
            pltpu.SemaphoreType.DMA((2, waves, count)),
            pltpu.VMEM((4,) + terms.shape, F32),
            pltpu.VMEM((2,) + terms.shape, F32),
            pltpu.VMEM((count,) + terms.shape, F32),
            pltpu.SemaphoreType.DMA((3 + count,)),
            pltpu.SemaphoreType.DMA((3 + count,)),
        ],
        compiler_params=pltpu.CompilerParams(
            collective_id=3, has_side_effects=True, vmem_limit_bytes=VMEM_LIMIT
        ),
        name="last_exchange",
    )(first_part, shrink_part, payload, terms, *extra)


def to_payload(rows):
    count, width = lax.axis_size("dp") // 2, rows.shape[1]
    piece = -(-rows.shape[0] // (WAVES * 2 * count * 16)) * 16
    padding = WAVES * 2 * count * piece - rows.shape[0]
    return jnp.pad(rows, ((0, padding), (0, 0))).reshape(WAVES, 2, count, piece, width)


def half_turn(array):
    columns = array.reshape(array.shape[0], -1, 2, HEAD_DIM // 2)
    return np.stack([-columns[:, :, 1], columns[:, :, 0]], axis=2).reshape(array.shape)


def turn_matrix(width):
    return jnp.asarray(half_turn(np.eye(width, dtype=np.float32)), BF16)


def rotary_tables(rows, heads):
    half_width = HEAD_DIM // 2
    frequency = THETA ** (-(jnp.arange(half_width, dtype=F32) * 2.0 / HEAD_DIM))
    angles = jnp.arange(SEQ_LEN, dtype=F32)[:, None] * frequency[None, :]
    angles = jnp.tile(angles, (1, 2 * heads))
    repeat = rows // SEQ_LEN
    return jnp.tile(jnp.cos(angles), (repeat, 1)), jnp.tile(jnp.sin(angles), (repeat, 1))


def on_device(
    tokens,
    first_gain,
    joint_weight,
    output_weight,
    second_gain,
    expand_weight,
    shrink_weight,
    cotangent,
):
    local_rows, model_width = tokens.shape
    own_rows = cotangent.shape[0]
    heads = joint_weight.shape[2] // HEAD_DIM
    inner = heads * HEAD_DIM
    units = expand_weight.shape[2]
    joint_flat = joint_weight.reshape(model_width, 3 * inner)
    expand_flat = expand_weight.reshape(model_width, 2 * units)
    gain_one_row = first_gain.reshape(1, model_width)
    gain_two_row = second_gain.reshape(1, model_width)
    turn = turn_matrix(inner)

    grad_rows = lax.all_gather(cotangent, "tensor", axis=0, tiled=True)

    first_hat, _ = norm_parts(tokens.astype(F32))
    normed = (first_hat * first_gain).astype(BF16)
    turned = [dot(joint_weight[:, part], turn).astype(BF16) for part in (0, 1)]
    joint = dot(normed, jnp.concatenate([joint_flat, *turned], axis=1))
    cosine, sine = rotary_tables(local_rows, heads)
    query = (joint[:, :inner] * cosine + joint[:, 3 * inner : 4 * inner] * sine).astype(BF16)
    query = query * jnp.asarray(SCALE, BF16)
    key = (joint[:, inner : 2 * inner] * cosine + joint[:, 4 * inner :] * sine).astype(BF16)
    value = joint[:, 2 * inner : 3 * inner].astype(BF16)
    query_t, key_t, value_t = query.T, key.T, value.T
    mixed_t, logsum = attend(key, query_t, value_t, heads, 256)
    branch_part = dot(mixed_t, output_weight, ((0,), (0,))).astype(BF16)
    second, middle = exchange(
        "middle_exchange",
        1,
        [branch_part],
        [tokens, gain_two_row],
        middle_step,
        [
            jax.ShapeDtypeStruct((local_rows, model_width), BF16),
            jax.ShapeDtypeStruct((own_rows, model_width), F32),
        ],
    )
    gate_up = dot(second, expand_flat)

    def activate(gate_part, up_part):
        return jax.nn.gelu(gate_part, approximate=True) * up_part

    hidden, activate_back = jax.vjp(activate, gate_up[:, :units], gate_up[:, units:])
    hidden = hidden.astype(BF16)
    grad_hidden = dot(grad_rows, shrink_weight, ((1,), (1,)))
    grad_gate, grad_up = activate_back(grad_hidden)
    grad_both = jnp.concatenate([grad_gate, grad_up], axis=1).astype(BF16)
    second_part = dot(grad_both, expand_flat, ((1,), (1,))).astype(BF16)
    grad_shrink = dot(hidden, grad_rows, ((0,), (0,))).astype(BF16)
    grad_expand = dot(second, grad_both, ((0,), (0,))).astype(BF16)
    second_part, grad_shrink, grad_expand = lax.optimization_barrier(
        (second_part, grad_shrink, grad_expand)
    )
    grad_shrink, grad_expand = lax.psum((grad_shrink, grad_expand), "dp")
    grad_branch, grad_middle, gain_two = exchange(
        "middle_back_exchange",
        2,
        [second_part],
        [middle, gain_two_row, cotangent],
        middle_back_step,
        [
            jax.ShapeDtypeStruct((local_rows, model_width), BF16),
            jax.ShapeDtypeStruct((own_rows, model_width), F32),
            jax.ShapeDtypeStruct((1, model_width), F32),
        ],
    )
    grad_mixed = dot(grad_branch, output_weight, ((1,), (1,))).astype(BF16)
    dq_t, dk, dv = attend_back(
        key, key_t, query, query_t, value, grad_mixed, grad_mixed.T, mixed_t, logsum, heads, 256
    )

    def turn_back(grad):
        return grad * cosine + dot((grad * sine).astype(BF16), turn, ((1,), (1,)))

    grad_joint = jnp.concatenate([turn_back(dq_t.T), turn_back(dk), dv], axis=1).astype(BF16)
    first_part = dot(grad_joint, joint_flat, ((1,), (1,)))
    gain_one = jnp.sum(first_part * first_hat, axis=0, keepdims=True)
    grad_joint_w = dot(grad_joint, normed, ((0,), (0,)))
    grad_output = dot(mixed_t, grad_branch)
    weights = jnp.concatenate([grad_joint_w, grad_output], axis=0).astype(BF16)
    gains = jnp.concatenate([gain_one, gain_two, jnp.zeros((6, model_width), F32)], axis=0)
    shrink_part = dot(hidden, shrink_weight).astype(BF16)
    grad_tokens, block_out, weights, gains = last_exchange(
        first_part.astype(BF16),
        shrink_part,
        to_payload(weights),
        gains,
        tokens,
        gain_one_row,
        middle,
        grad_middle,
    )
    weights = weights.reshape(-1, model_width)
    grad_joint_w = weights[: 3 * inner].astype(F32).T
    return (
        block_out,
        grad_tokens,
        gains[0],
        grad_joint_w.reshape(model_width, 3, inner),
        weights[3 * inner : 4 * inner].astype(F32),
        gains[1],
        grad_expand.astype(F32).reshape(model_width, 2, units),
        grad_shrink.astype(F32),
    )


def solution(mesh):
    return jax.shard_map(
        on_device,
        mesh=mesh,
        in_specs=(
            P("dp", None),
            P(),
            P(None, None, "tensor"),
            P("tensor", None),
            P(),
            P(None, None, "tensor"),
            P("tensor", None),
            P(("dp", "tensor"), None),
        ),
        out_specs=(
            P(("dp", "tensor"), None),
            P(("dp", "tensor"), None),
            P(),
            P(None, None, "tensor"),
            P("tensor", None),
            P(),
            P(None, None, "tensor"),
            P("tensor", None),
        ),
        check_vma=False,
    )
```

time: 308 us -> 234 us (0.76)
  waiting for transfers between devices: 102 us -> 34.3 us
  Pallas kernels: 96.9 us -> 119 us
  blocking collectives: 19.9 us -> 0 us
  other arithmetic: 14.8 us -> 11.7 us
    psum x1, waiting for transfers between devices: 71.3 us -> 33.6 us  [on_device(): grad_shrink, grad_expand = lax.psum((grad_shrink, grad_expand), 'dp')]
    psum x1 -> x0, waiting for transfers between devices: 29.5 us -> none  [on_device(): lax.psum((grad_joint_w, grad_output, gains), 'dp')]
    pallas_call x4 -> x3, Pallas kernels: 74.4 us -> 99.6 us  [the longest x1 53.7 us: last_exchange(): pl.pallas_call(functools.partial(last_kernel, own), in_specs=[VMEM] * 8,...]
    psum x1 -> x0, blocking collectives: 19.9 us -> none  [on_device(): lax.psum((grad_joint_w, grad_output, gains), 'dp')]
    convert_element_type x3 -> x2, other arithmetic: 5.59 us -> 1.79 us  [the longest x1 0.93 us: on_device(): (joint[:, inner:2 * inner] * cosine + joint[:, 4 * inner:] * sine).astype...]
    unnamed x97 -> x83, local copies, waits for them, and re-layouts: 20.1 us -> 18.4 us
  transfers between devices with their start and end apart: 3 -> 2, of which waited for: 2 -> 1; matrix products, arithmetic and copies ran while one was open for 11% -> 9% of each run, Pallas kernels for 20% -> 37%
where the time goes in v2:
time: 234 us; the launch traced here: 233 us
  Pallas kernels  119 us (51%)
  waiting for transfers between devices  34.3 us (15%)
  local copies, waits for them, and re-layouts  27.6 us (12%)
  matrix products  26.1 us (11%)
  between operations  14.5 us (6%)
  other arithmetic  11.7 us (5%)
    pallas_call x1, Pallas kernels, last_exchange(): pl.pallas_call(functools.partial(last_kernel, own), in_specs=[VMEM] * 8,...  53.7 us
    pallas_call x2, Pallas kernels, exchange(): pl.pallas_call(functools.partial(exchange_kernel, sums, len(extra), step,...  46 us
    psum x1, waiting for transfers between devices, on_device(): grad_shrink, grad_expand = lax.psum((grad_shrink, grad_expand), 'dp')  33.6 us
    dot_general x16, matrix products, dot(): return lax.dot_general(a, b, (dims, ((), ())), preferred_element_type=F32)  26.1 us
    unnamed x83, local copies, waits for them, and re-layouts  18.4 us
    pallas_call x1, Pallas kernels, attend_back(): pl.pallas_call(functools.partial(attend_back_kernel, heads, per_seq), gri...  11.1 us
    pallas_call x1, Pallas kernels, attend(): pl.pallas_call(functools.partial(attend_kernel, heads), grid=(rows // blo...  8.52 us
  transfers between devices with their start and end apart: 2, of which 1 were waited for; matrix products, arithmetic and copies ran while one was open for 9% of the time, Pallas kernels for 37%

profile of v2, /device:TPU:0, one launch (start us, length us, event | category | flops | bytes accessed | tf_op | source)
XLA Modules:
  0.0 233.5 jit_solution(13503904020116626273)
XLA Ops:
  8.0 1.8 convert_reduce_fusion
  11.6 1.9 fusion.7
  13.5 0.9 fusion.25
  15.1 2.0 copy.29.key
  17.1 1.0 copy.35.value
  18.1 1.0 copy.30.query
  19.2 1.0 copy-done.5
  20.3 8.5 %attend.1 = (bf16[192,1024]{1,0:T(8,128)(2,1)S(1)}, f32[8,1024]{1,0:T(8,128)S(1)}) custom-call(bf16[1024,192]{1,0:T(8,128)(2,1)S(1)} %copy-done.5, bf16[192,1024]{1,0:T(8,128)(2,1)S(1)} %bitcast.82, bf16[192,1024]{1,0:T(8,128)(2,1)S(1)} %bitcast.84), custom_call_target="tpu_custom_call" | custom-call | tf_op jit(solution)/shard_map/attend/pallas_call | solution.py:67
  28.8 1.6 convolution_convert_fusion.2.refs_0_
  30.4 0.7 copy-done.10
  31.1 23.4 %middle_exchange.1 = (bf16[1024,768]{1,0:T(8,128)(2,1)S(1)}, f32[256,768]{1,0:T(8,128)S(1)}) custom-call(bf16[1024,768]{1,0:T(8,128)(2,1)S(1)} %convolution_convert_fusion.2.refs_0_, bf16[1024,768]{1,0:T(8,128)(2,1)S(1)} %copy-done.1, f32[1,768]{1,0:T(1,128)S(1)} %reshape.89.refs_2_), custom_call_target="tpu_custom_call" | custom-call | tf_op jit(solution)/shard_map/middle_exchange/pallas_call | solution.py:289
  54.6 0.9 copy-done.2
  55.5 1.1 copy-done.22
  56.6 2.5 %fusion.46 = f32[1024,576]{0,1:T(8,128)} fusion(bf16[1024,768]{1,0:T(8,128)(2,1)S(1)} %get-tuple-element.26, bf16[768,576]{0,1:T(8,128)(2,1)S(1)} %bitcast.79), kind=kOutput, calls=%fused_computation.84 | convolution fusion | flops 905969664 | bytes 4816896 | tf_op jit(solution)/shard_map/dot_general | solution.py:25
  59.1 3.7 %fusion.21 = (bf16[1024,288]{0,1:T(8,128)(2,1)S(1)}, bf16[1024,288]{0,1:T(8,128)(2,1)S(1)}, bf16[1024,288]{0,1:T(8,128)(2,1)S(1)}) fusion(f32[1024,576]{0,1:T(8,128)} %fusion.46, bf16[1024,768]{1,0:T(8,128)(2,1)} %all-gather.2.cloned.1.call-done, bf16[288,768]{1,0:T(8,128)(2,1)} %param.15), kind=kOutput, calls=%fused_computation.45 | convolution fusion | flops 460652544 | bytes 6144000 | tf_op jit(solution)/shard_map/dot_general | solution.py:25
  62.9 2.0 convolution_convert_fusion.3
  64.9 1.4 convolution_convert_fusion.refs_0_
  66.4 1.4 convolution_convert_fusion.5
  67.8 22.5 %middle_back_exchange.1 = (bf16[1024,768]{1,0:T(8,128)(2,1)S(1)}, f32[256,768]{1,0:T(8,128)S(1)}, f32[1,768]{1,0:T(1,128)S(1)}) custom-call(bf16[1024,768]{1,0:T(8,128)(2,1)S(1)} %convolution_convert_fusion.refs_0_, f32[256,768]{1,0:T(8,128)S(1)} %copy-done.3, f32[1,768]{1,0:T(1,128)S(1)} %reshape.89.refs_2_, bf16[256,768]{1,0:T(8,128)(2,1)S(1)} %copy-done.9), custom_call_target="tpu_custom_call" | custom-call | tf_op jit(solution)/shard_map/middle_back_exchange/pallas_call | solution.py:289
  90.3 0.9 copy-done.16
  91.2 1.1 copy-done.7
  92.4 1.4 convolution_convert_fusion.6
  93.8 2.0 copy.31.grad
  95.8 1.0 copy-done.8
  96.8 1.0 copy-done.11
  97.8 1.0 copy-done.18
  98.8 1.0 copy-done.19
  99.9 1.0 copy-done.20
  100.9 1.0 copy-done.21
  101.9 11.1 %attend_back.1 = (f32[192,1024]{1,0:T(8,128)S(1)}, f32[1024,192]{1,0:T(8,128)S(1)}, f32[1024,192]{1,0:T(8,128)}) custom-call(bf16[1024,192]{1,0:T(8,128)(2,1)S(1)} %copy-done.6, bf16[192,1024]{1,0:T(8,128)(2,1)S(1)} %bitcast.85, bf16[1024,192]{1,0:T(8,128)(2,1)S(1)} %copy-done.19, bf16[192,1024]{1,0:T(8,128)(2,1)S(1)} %bitcast.83, ...), custom_call_target="tpu_custom_call" | custom-call | flops 3221225472 | bytes 3145728 | tf_op jit(solution)/shard_map/attend_back/pallas_call | solution.py:117
  113.0 1.0 copy-done.13
  114.0 0.9 copy-done.15
  114.9 2.2 copy.34
  117.1 1.2 copy.32
  118.3 1.7 fusion.29
  121.1 2.2 convolution_convert_fusion.4
  123.3 2.7 %fusion.5 = (f32[768]{0:T(1024)S(1)}, bf16[1024,768]{1,0:T(8,128)(2,1)}) fusion(bf16[1024,768]{1,0:T(8,128)(2,1)S(1)} %copy-done.1, f32[1024]{0:T(1024)S(1)} %add_rsqrt_fusion, f32[1024]{0:T(1024)S(1)} %broadcast_multiply_fusion, bf16[768,576]{0,1:T(8,128)(2,1)S(1)} %bitcast.92, bf16[1024,192]{0,1:T(8,128)(2,1)S(1)} %copy-done.30, ...), kind=kOutput, calls=%fused_computation.7 | convolution fusion | flops 914226432 | bytes 5221376 | tf_op jit(solution)/shard_map/dot_general | solution.py:25
  126.1 2.0 convolution_convert_fusion.7
  128.3 0.8 copy-done.37
  129.2 2.2 convolution_convert_fusion.1.refs_1_
  131.4 53.7 %last_exchange.1 = (f32[256,768]{1,0:T(8,128)S(1)}, bf16[256,768]{1,0:T(8,128)(2,1)S(1)}, bf16[2,2,4,48,768]{4,3,2,1,0:T(8,128)(2,1)S(1)}, f32[8,768]{1,0:T(8,128)S(1)}) custom-call(bf16[1024,768]{1,0:T(8,128)(2,1)} %get-tuple-element.51.refs_0_, bf16[1024,768]{1,0:T(8,128)(2,1)} %convolution_convert_fusion.1.refs_1_, ...), custom_call_target="tpu_custom_call" | custom-call | tf_op jit(solution)/shard_map/last_exchange/pallas_call | solution.py:507
  185.7 0.9 slice_convert_fusion.2
  186.6 1.3 slice_convert_fusion
  187.9 33.6 %all-reduce.3.cloned.1.call-done = (bf16[768,2,288]{0,2,1:T(8,128)(2,1)}, bf16[288,768]{1,0:T(8,128)(2,1)}) async-done(((bf16[768,2,288]{0,2,1:T(8,128)(2,1)}, bf16[288,768]{1,0:T(8,128)(2,1)}), (bf16[768,2,288]{0,2,1:T(8,128)(2,1)}, bf16[288,768]{1,0:T(8,128)(2,1)})) %all-reduce.3.cloned.1.call-update) | async-done | bytes 1327120 | tf_op jit(solution)/shard_map/psum | solution.py:626
  221.5 2.6 %reshape.95 = f32[768,2,288]{0,2,1:T(8,128)} convert(bf16[768,2,288]{0,2,1:T(8,128)(2,1)} %get-tuple-element.44) | non-fusion elementwise | flops 442368 | bytes 2654208 | tf_op jit(solution)/shard_map/reshape | solution.py:674
  224.0 1.0 convert_element_type.85
  225.0 0.7 copy.41
  225.7 0.9 copy.42
  (88 shorter events, 5.3 us)
Async XLA Ops:
  7.2 48.3 %copy-start = (bf16[768,2,288]{0,2,1:T(8,128)(2,1)S(1)}, bf16[768,2,288]{0,2,1:T(8,128)(2,1)}, u32[]{:S(2)}) copy-start(bf16[768,2,288]{0,2,1:T(8,128)(2,1)} %param.14) | copy-start | bytes 2654212
  7.2 2.6 %copy-start.1 = (bf16[1024,768]{1,0:T(8,128)(2,1)S(1)}, bf16[1024,768]{1,0:T(8,128)(2,1)}, u32[]{:S(2)}) copy-start(bf16[1024,768]{1,0:T(8,128)(2,1)} %refs_4_.1) | copy-start | bytes 4718596
  7.2 2.6 %copy-start.35 = (f32[768]{0:T(1024)S(1)}, f32[768]{0:T(1024)}, u32[]{:S(2)}) copy-start(f32[768]{0:T(1024)} %param.10) | copy-start | bytes 9220
  7.2 51.9 %all-gather.2.cloned.1.call-start = ((), (), s32[]{:S(2)}) async-start(), calls=%async_computation | async-start | bytes 1966080 | tf_op jit(solution)/shard_map/all_gather | solution.py:585
  7.9 3.1 %copy-start.26 = (bf16[192,192]{1,0:T(8,128)(2,1)S(1)}, bf16[192,192]{1,0:T(8,128)(2,1)}, u32[]{:S(2)}) copy-start(bf16[192,192]{1,0:T(8,128)(2,1)} %constant.33.clone) | copy-start | bytes 221188
  8.0 213.5 %all-reduce.3.cloned.1.call-start = ((), (), s32[]{:S(2)}) async-start(), calls=%async_computation.1 | async-start | bytes 2654208 | tf_op jit(solution)/shard_map/psum | solution.py:626
  8.0 3.0 %copy-start.31 = (bf16[768,3,192]{0,2,1:T(8,128)(2,1)S(1)}, bf16[768,3,192]{0,2,1:T(8,128)(2,1)}, u32[]{:S(2)}) copy-start(bf16[768,3,192]{0,2,1:T(8,128)(2,1)} %param.11) | copy-start | bytes 2654212
  11.0 3.4 %copy-start.24 = (f32[1024,32]{0,1:T(8,128)}, f32[1024,32]{0,1:T(8,128)S(1)}, u32[]{:S(2)}) copy-start(f32[1024,32]{0,1:T(8,128)S(1)} %get-tuple-element.59) | copy-start | bytes 393220
  11.0 3.4 %copy-start.25 = (f32[1024,32]{0,1:T(8,128)}, f32[1024,32]{0,1:T(8,128)S(1)}, u32[]{:S(2)}) copy-start(f32[1024,32]{0,1:T(8,128)S(1)} %get-tuple-element.60) | copy-start | bytes 393220
  14.4 0.7 copy-start.34
  19.2 1.1 copy-start.5
  30.4 0.7 copy-start.10
  54.6 0.9 copy-start.2
  55.5 1.1 copy-start.22
  59.1 3.7 %copy-start.23 = (bf16[1024,768]{1,0:T(8,128)(2,1)S(1)}, bf16[1024,768]{1,0:T(8,128)(2,1)}, u32[]{:S(2)}) copy-start(bf16[1024,768]{1,0:T(8,128)(2,1)} %copy-done.22) | copy-start | bytes 4718596
  62.9 3.5 %copy-start.38 = (bf16[1024,288]{0,1:T(8,128)(2,1)}, bf16[1024,288]{0,1:T(8,128)(2,1)S(1)}, u32[]{:S(2)}) copy-start(bf16[1024,288]{0,1:T(8,128)(2,1)S(1)} %get-tuple-element.52) | copy-start | bytes 1769476
  64.9 1.5 copy-start.36
  66.4 1.4 copy-start.3
  66.4 1.4 copy-start.9
  67.8 24.6 %copy-start.33 = (bf16[192,768]{1,0:T(8,128)(2,1)S(1)}, bf16[192,768]{1,0:T(8,128)(2,1)}, u32[]{:S(2)}) copy-start(bf16[192,768]{1,0:T(8,128)(2,1)} %param.12) | copy-start | bytes 884740
  90.3 0.9 copy-start.16
  91.2 1.1 copy-start.7
  92.4 3.4 %copy-start.6 = (bf16[1024,192]{1,0:T(8,128)(2,1)S(1)}, bf16[1024,192]{1,0:T(8,128)(2,1)}, u32[]{:S(2)}) copy-start(bf16[1024,192]{1,0:T(8,128)(2,1)} %copy.29.key) | copy-start | bytes 1179652
  95.8 1.0 copy-start.8
  96.8 1.0 copy-start.11
  97.8 1.0 copy-start.18
  98.8 1.0 copy-start.19
  99.9 1.0 copy-start.20
  100.9 1.0 copy-start.21
  113.0 1.0 copy-start.13
  114.0 0.9 copy-start.15
  114.9 2.3 copy-start.14
  118.3 1.8 copy-start.27
  120.1 1.0 copy-start.30
  121.1 2.2 copy-start.32
  123.3 2.8 %copy-start.12 = (bf16[192,1024]{1,0:T(8,128)(2,1)S(1)}, bf16[192,1024]{1,0:T(8,128)(2,1)}, u32[]{:S(2)}) copy-start(bf16[192,1024]{1,0:T(8,128)(2,1)} %copy-done.10) | copy-start | bytes 1179652
  126.0 2.0 copy-start.28
  128.0 1.0 copy-start.37
  128.1 1.2 copy-start.39
  128.2 3.2 %copy-start.4 = (f32[256,768]{1,0:T(8,128)S(1)}, f32[256,768]{1,0:T(8,128)}, u32[]{:S(2)}) copy-start(f32[256,768]{1,0:T(8,128)} %copy-done.2) | copy-start | bytes 2359300
  128.2 3.2 %copy-start.17 = (f32[256,768]{1,0:T(8,128)S(1)}, f32[256,768]{1,0:T(8,128)}, u32[]{:S(2)}) copy-start(f32[256,768]{1,0:T(8,128)} %copy-done.16) | copy-start | bytes 2359300
  221.5 2.6 %copy-start.29 = (bf16[288,768]{1,0:T(8,128)(2,1)S(1)}, bf16[288,768]{1,0:T(8,128)(2,1)}, u32[]{:S(2)}) copy-start(bf16[288,768]{1,0:T(8,128)(2,1)} %get-tuple-element.45) | copy-start | bytes 1327108
Sparse Core Ops, SparseCore 0:
  9.6 22.3 all-gather.1
  126.2 95.2 all-reduce.2

commit v3 on v2

--- a/solution.py
+++ b/solution.py
@@ -85,63 +85,6 @@
     )(key, query_t, value_t)
 
 
-def attend_back_kernel(
-    heads, per_seq, key, key_t, query, query_t, value, grad, grad_t, mixed_t, logsum, dq_t, dk, dv
-):
-    @pl.when(pl.program_id(0) % per_seq == 0)
-    def _():
-        dk[...] = jnp.zeros_like(dk)
-        dv[...] = jnp.zeros_like(dv)
-
-    for head in range(heads):
-        rows = slice(head * HEAD_DIM, (head + 1) * HEAD_DIM)
-        scores = dot(key[...], head_rows(query_t[...], head))
-        probs = jnp.exp(scores - logsum[head : head + 1, :])
-        dprobs = dot(value[...], head_rows(grad_t[...], head))
-        delta = jnp.sum(
-            grad_t[rows, :].astype(F32) * mixed_t[rows, :].astype(F32), axis=0, keepdims=True
-        )
-        dscores = (probs * (dprobs - delta)).astype(BF16)
-        dq_t[rows, :] = dot(key_t[rows, :], dscores) * SCALE
-        dk[...] += dot(dscores, head_columns(query[...], head))
-        dv[...] += dot(probs.astype(BF16), head_columns(grad[...], head))
-
-
-def attend_back(key, key_t, query, query_t, value, grad, grad_t, mixed_t, logsum, heads, block):
-    width, rows = query_t.shape
-    per_seq = SEQ_LEN // block
-    seq_down = pl.BlockSpec((SEQ_LEN, width), lambda i: (i // per_seq, 0))
-    seq_across = pl.BlockSpec((width, SEQ_LEN), lambda i: (0, i // per_seq))
-    down = pl.BlockSpec((block, width), lambda i: (i, 0))
-    across = pl.BlockSpec((width, block), lambda i: (0, i))
-    return pl.pallas_call(
-        functools.partial(attend_back_kernel, heads, per_seq),
-        grid=(rows // block,),
-        in_specs=[
-            seq_down,
-            seq_across,
-            down,
-            across,
-            seq_down,
-            down,
-            across,
-            across,
-            pl.BlockSpec((8, block), lambda i: (0, i)),
-        ],
-        out_specs=[across, seq_down, seq_down],
-        out_shape=[
-            jax.ShapeDtypeStruct((width, rows), F32),
-            jax.ShapeDtypeStruct((rows, width), F32),
-            jax.ShapeDtypeStruct((rows, width), F32),
-        ],
-        compiler_params=pltpu.CompilerParams(vmem_limit_bytes=VMEM_LIMIT),
-        cost_estimate=pl.CostEstimate(
-            flops=16 * rows * SEQ_LEN * width, bytes_accessed=16 * rows * width, transcendentals=0
-        ),
-        name="attend_back",
-    )(key, key_t, query, query_t, value, grad, grad_t, mixed_t, logsum)
-
-
 def remote(src, dst, send_sem, recv_sem, target):
     copy = pltpu.make_async_remote_copy(
         src_ref=src,
@@ -234,9 +177,9 @@
             + self.from_side[slot, here].astype(F32)
         )
 
-    def finish(self, step, extra, outs):
+    def totals(self, step, extra, outs):
         sums = len(self.parts)
-        gathered = []
+        self.gathered = []
         for chunk in range(CHUNKS):
             totals = [self.total(slot, chunk) for slot in range(sums)]
             result = step(chunk, self.at(self.me, chunk), self.here(chunk), totals, extra, outs)
@@ -244,13 +187,17 @@
                 outs[0][self.at(self.me, chunk), :] = result
                 block = outs[0].at[self.at(self.me, chunk)]
                 over = self.over(block, block, sums, chunk)
-                gathered.append((over, self.to_core(block, block, 2 * sums, chunk)))
+                near = self.to_core(block, block, 2 * sums, chunk)
+                self.gathered.append((over, near))
+
+    def spread(self, whole):
+        sums = len(self.parts)
         relayed = []
-        for chunk, (over, _) in enumerate(gathered):
+        for chunk, (over, _) in enumerate(self.gathered):
             over.wait_recv()
-            block = outs[0].at[self.at(self.side_peer, chunk)]
+            block = whole.at[self.at(self.side_peer, chunk)]
             relayed.append(self.to_core(block, block, 2 * sums + 1, chunk))
-        for _, near in gathered:
+        for _, near in self.gathered:
             near.wait_recv()
         for relay in relayed:
             relay.wait_recv()
@@ -265,7 +212,9 @@
     greet(work.peers())
     work.start()
     work.cross_over()
-    work.finish(step, refs[sums : sums + extras], refs[sums + extras : -7])
+    outs = refs[sums + extras : -7]
+    work.totals(step, refs[sums : sums + extras], outs)
+    work.spread(outs[0])
     work.close()
 
 
@@ -322,13 +271,14 @@
     return value.astype(BF16)
 
 
-def last_step(chunk, rows, here, totals, extra, outs):
-    tokens, gain, middle, grad_middle = extra
-    grad_tokens, block_out = outs
+def token_step(chunk, rows, here, totals, extra, outs):
+    tokens, gain, grad_middle = extra
     hat, inverse = norm_parts(tokens[rows, :].astype(F32))
-    grad_tokens[here, :] = grad_middle[here, :] + norm_back(hat, inverse, gain[...], totals[0])
-    block_out[here, :] = (middle[here, :] + totals[1]).astype(BF16)
-    return None
+    outs[0][here, :] = grad_middle[here, :] + norm_back(hat, inverse, gain[...], totals[0])
+
+
+def out_step(chunk, rows, here, totals, extra, outs):
+    outs[0][here, :] = (extra[0][here, :] + totals[0]).astype(BF16)
 
 
 class DataSum:
@@ -336,7 +286,7 @@
         self.payload, self.result = payload, total
         self.from_pair, self.summed, self.arrived = scratch[:3]
         self.pair_send, self.pair_recv, self.far_send, self.far_recv = scratch[3:]
-        self.waves, _, self.count = payload.shape[:3]
+        self.waves, self.count = WAVES, payload.shape[0] // (2 * WAVES)
         data = lax.axis_index("dp")
         self.outer, self.inner = data // 2, data % 2
         self.unsent = []
@@ -349,6 +299,9 @@
 
     def peers(self):
         return [self.pair()] + [self.far(hop) for hop in range(1, self.count)]
+
+    def unit(self, wave, inner, outer):
+        return (wave * 2 + inner) * self.count + outer
 
     def place(self, hop):
         return (self.outer + hop) % self.count
@@ -372,7 +325,7 @@
     def start(self):
         self.near = {
             (wave, hop): self.to_pair(
-                self.payload.at[wave, 1 - self.inner, self.place(hop)],
+                self.payload.at[self.unit(wave, 1 - self.inner, self.place(hop))],
                 self.from_pair.at[wave, hop],
                 0,
                 wave,
@@ -388,7 +341,7 @@
         for hop in self.hops():
             self.near[wave, hop].wait_recv()
             self.summed[wave, hop] = (
-                self.payload[wave, self.inner, self.place(hop)].astype(F32)
+                self.payload[self.unit(wave, self.inner, self.place(hop))].astype(F32)
                 + self.from_pair[wave, hop].astype(F32)
             ).astype(BF16)
             if hop:
@@ -401,8 +354,8 @@
         for hop in range(1, self.count):
             self.spread[wave, hop].wait_recv()
             value = value + self.arrived[wave, hop - 1].astype(F32)
-        self.result[wave, self.inner, self.outer] = value.astype(BF16)
-        block = self.result.at[wave, self.inner, self.outer]
+        self.result[self.unit(wave, self.inner, self.outer)] = value.astype(BF16)
+        block = self.result.at[self.unit(wave, self.inner, self.outer)]
         for hop in range(1, self.count):
             self.shared[wave, hop] = self.to_far(block, block, hop, 1, wave, hop)
         self.shared[wave, 0] = self.to_pair(block, block, 1, wave, 0)
@@ -410,7 +363,7 @@
     def relay(self, wave):
         for hop in range(1, self.count):
             self.shared[wave, hop].wait_recv()
-            block = self.result.at[wave, self.inner, self.behind(hop)]
+            block = self.result.at[self.unit(wave, self.inner, self.behind(hop))]
             self.near[wave, hop] = self.to_pair(block, block, 1, wave, hop)
 
     def finish(self):
@@ -472,75 +425,202 @@
             copy.wait_send()
 
 
-def last_kernel(own, *refs):
-    first_part, shrink_part, payload, terms, *extra = refs[:8]
-    grad_tokens, block_out, summed, gains = refs[8:12]
-    scratch = refs[12:]
-    group = GroupSum((first_part, shrink_part), own, False, scratch[:7])
-    data = DataSum(payload, summed, scratch[7:14])
-    gain = GainSum(terms, gains, group, data, scratch[14:])
-    greet(group.peers() + [{"tensor": group.cross}] + data.peers())
-    data.start()
+def back_kernel(heads, own, count, *refs):
+    (
+        second_part,
+        shrink_part,
+        early_part,
+        tokens,
+        gain_one,
+        gain_two,
+        middle,
+        cotangent,
+        output_weight,
+        joint,
+        normed,
+        cosine,
+        sine,
+        turn,
+        key,
+        key_t,
+        query,
+        query_t,
+        value,
+        mixed_t,
+        logsum,
+    ) = refs[:21]
+    block_out, grad_tokens, early_sum, late_sum, gains = refs[21:26]
+    grad_branch, grad_middle, term_two, first_part, late_part, terms = refs[26:32]
+    grad_mixed, grad_mixed_t, dq_t, dk, dv = refs[32:37]
+    scratch = refs[37:]
+    rows, width = tokens.shape
+    inner = heads * HEAD_DIM
+    block = 256
+
+    norm_sum = GroupSum((second_part,), own, True, scratch[:7])
+    out_sum = GroupSum((shrink_part,), own, False, scratch[7:14])
+    token_sum = GroupSum((first_part,), own, False, scratch[14:21])
+    early = DataSum(early_part, early_sum, scratch[21:28])
+    late = DataSum(late_part, late_sum, scratch[28:35])
+    gain = GainSum(terms, gains, norm_sum, early, scratch[35:40])
+    greet(norm_sum.peers() + [{"tensor": norm_sum.cross}] + early.peers())
+
+    norm_sum.start()
+    early.start()
+    norm_sum.cross_over()
+    early.scatter(0)
+    norm_sum.totals(
+        middle_back_step,
+        (middle, gain_two, cotangent),
+        (grad_branch, grad_middle, term_two),
+    )
+    early.scatter(1)
+    early.collect(0)
+    norm_sum.spread(grad_branch)
+    out_sum.start()
+    early.collect(1)
+
+    grad_mixed[...] = dot(grad_branch[...], output_weight[...], ((1,), (1,))).astype(BF16)
+    grad_mixed_t[...] = dot(output_weight[...], grad_branch[...], ((1,), (1,))).astype(BF16)
+    dk[...] = jnp.zeros_like(dk)
+    dv[...] = jnp.zeros_like(dv)
+
+    def attend_rows(number, carry):
+        down = pl.ds(pl.multiple_of(number * block, block), block)
+        for head in range(heads):
+            part = slice(head * HEAD_DIM, (head + 1) * HEAD_DIM)
+            scores = dot(key[...], head_rows(query_t[:, down], head))
+            probs = jnp.exp(scores - logsum[head : head + 1, down])
+            grad_t = grad_mixed_t[:, down]
+            dprobs = dot(value[...], head_rows(grad_t, head))
+            delta = jnp.sum(
+                grad_mixed_t[part, down].astype(F32) * mixed_t[part, down].astype(F32),
+                axis=0,
+                keepdims=True,
+            )
+            dscores = (probs * (dprobs - delta)).astype(BF16)
+            dq_t[part, down] = dot(key_t[part, :], dscores) * SCALE
+            dk[...] += dot(dscores, head_columns(query[down, :], head))
+            dv[...] += dot(probs.astype(BF16), head_columns(grad_mixed[down, :], head))
+        return carry
+
+    blocks = rows // block
+    lax.fori_loop(0, blocks // 2, attend_rows, 0)
+    out_sum.cross_over()
+    early.relay(0)
+    lax.fori_loop(blocks // 2, blocks, attend_rows, 0)
+    early.relay(1)
+
+    def turn_back(grad):
+        moved = dot((grad * sine[...]).astype(BF16), turn[...], ((1,), (1,)))
+        return (grad * cosine[...] + moved).astype(BF16)
+
+    grad_parts = (turn_back(dq_t[...].T[:, :inner]), turn_back(dk[...]), dv[...].astype(BF16))
+    gain_term = jnp.zeros((1, width), F32)
+    for owner in range(rows // own):
+        here = slice(owner * own, (owner + 1) * own)
+        value_rows = sum(
+            dot(grad_parts[part][here], joint[part], ((1,), (1,))) for part in range(3)
+        )
+        first_part[here, :] = value_rows.astype(BF16)
+        gain_term += jnp.sum(value_rows * normed[here, :].astype(F32), axis=0, keepdims=True)
+    token_sum.start()
+    terms[...] = jnp.zeros_like(terms)
+    terms[0:1, :] = gain_term / gain_one[...]
+    terms[1:2, :] = term_two[...]
     gain.start()
-    group.start()
-    group.cross_over()
+
+    units, piece, _ = late_part.shape
+    step = inner // piece
+    for part in range(3):
+        grad_weight = dot(grad_parts[part], normed[...], ((0,), (0,))).astype(BF16)
+        late_part[part * step : (part + 1) * step] = grad_weight.reshape(step, piece, width)
+    grad_output = dot(mixed_t[...], grad_branch[...]).astype(BF16)
+    late_part[3 * step : 4 * step] = grad_output.reshape(step, piece, width)
+    if units > 4 * step:
+        late_part[4 * step :] = jnp.zeros((units - 4 * step, piece, width), BF16)
+    late.start()
+    token_sum.cross_over()
     gain.pair_up()
-    for wave in range(data.waves):
-        data.scatter(wave)
-        if wave:
-            data.collect(wave - 1)
-    data.collect(data.waves - 1)
+    out_sum.totals(out_step, (middle,), (block_out,))
+    early.finish()
+    late.scatter(0)
+    late.scatter(1)
+    late.collect(0)
     gain.spread()
-    group.finish(last_step, extra, (grad_tokens, block_out))
-    for wave in range(data.waves):
-        data.relay(wave)
+    late.collect(1)
+    token_sum.totals(token_step, (tokens, gain_one, grad_middle), (grad_tokens,))
+    late.relay(0)
+    late.relay(1)
     gain.finish()
-    data.finish()
-    for work in (group, data, gain):
+    late.finish()
+    for work in (norm_sum, out_sum, token_sum, early, late, gain):
         work.close()
 
 
-def last_exchange(first_part, shrink_part, payload, terms, *extra):
-    own, width = first_part.shape[0] // 4, first_part.shape[1]
-    waves, _, count, rows, _ = payload.shape
-    pieces = (waves, count, rows, width)
+def sum_scratch(units, piece, width, count):
+    held = pltpu.VMEM((WAVES, count, piece, width), BF16)
+    return [held] * 3 + [pltpu.SemaphoreType.DMA((2, WAVES, count))] * 4
+
+
+def piece_rows(rows, count):
+    return -(-rows // (WAVES * 2 * count * 16)) * 16
+
+
+def back(second_part, shrink_part, early_part, *rest, heads, own):
+    rows, width = second_part.shape
+    count = lax.axis_size("dp") // 2
+    inner = heads * HEAD_DIM
+    early_shape = early_part.shape
+    late_shape = (WAVES * 2 * count, piece_rows(4 * inner, count), width)
+    padded = -(-inner // 128) * 128
     return pl.pallas_call(
-        functools.partial(last_kernel, own),
-        in_specs=[VMEM] * 8,
-        out_specs=[VMEM] * 4,
+        functools.partial(back_kernel, heads, own, count),
+        in_specs=[VMEM] * 21,
+        out_specs=[VMEM] * 5,
         out_shape=[
+            jax.ShapeDtypeStruct((own, width), BF16),
             jax.ShapeDtypeStruct((own, width), F32),
-            jax.ShapeDtypeStruct((own, width), BF16),
-            jax.ShapeDtypeStruct(payload.shape, BF16),
-            jax.ShapeDtypeStruct(terms.shape, F32),
+            jax.ShapeDtypeStruct(early_shape, BF16),
+            jax.ShapeDtypeStruct(late_shape, BF16),
+            jax.ShapeDtypeStruct((8, width), F32),
         ],
         scratch_shapes=[
-            *exchange_scratch(2, own, width, False),
-            pltpu.VMEM(pieces, BF16),
-            pltpu.VMEM(pieces, BF16),
-            pltpu.VMEM(pieces, BF16),
-            pltpu.SemaphoreType.DMA((2, waves, count)),
-            pltpu.SemaphoreType.DMA((2, waves, count)),
-            pltpu.SemaphoreType.DMA((2, waves, count)),
-            pltpu.SemaphoreType.DMA((2, waves, count)),
-            pltpu.VMEM((4,) + terms.shape, F32),
-            pltpu.VMEM((2,) + terms.shape, F32),
-            pltpu.VMEM((count,) + terms.shape, F32),
+            pltpu.VMEM((rows, width), BF16),
+            pltpu.VMEM((own, width), F32),
+            pltpu.VMEM((1, width), F32),
+            pltpu.VMEM((rows, width), BF16),
+            pltpu.VMEM(late_shape, BF16),
+            pltpu.VMEM((8, width), F32),
+            pltpu.VMEM((rows, inner), BF16),
+            pltpu.VMEM((inner, rows), BF16),
+            pltpu.VMEM((padded, rows), F32),
+            pltpu.VMEM((rows, inner), F32),
+            pltpu.VMEM((rows, inner), F32),
+            *exchange_scratch(1, own, width, True),
+            *exchange_scratch(1, own, width, False),
+            *exchange_scratch(1, own, width, False),
+            *sum_scratch(*early_shape, count),
+            *sum_scratch(*late_shape, count),
+            pltpu.VMEM((4, 8, width), F32),
+            pltpu.VMEM((2, 8, width), F32),
+            pltpu.VMEM((count, 8, width), F32),
             pltpu.SemaphoreType.DMA((3 + count,)),
             pltpu.SemaphoreType.DMA((3 + count,)),
         ],
         compiler_params=pltpu.CompilerParams(
-            collective_id=3, has_side_effects=True, vmem_limit_bytes=VMEM_LIMIT
+            collective_id=3, has_side_effects=True, vmem_limit_bytes=56 * 1024 * 1024
         ),
-        name="last_exchange",
-    )(first_part, shrink_part, payload, terms, *extra)
+        name="back",
+    )(second_part, shrink_part, early_part, *rest)
 
 
 def to_payload(rows):
     count, width = lax.axis_size("dp") // 2, rows.shape[1]
-    piece = -(-rows.shape[0] // (WAVES * 2 * count * 16)) * 16
-    padding = WAVES * 2 * count * piece - rows.shape[0]
-    return jnp.pad(rows, ((0, padding), (0, 0))).reshape(WAVES, 2, count, piece, width)
+    piece = piece_rows(rows.shape[0], count)
+    units = WAVES * 2 * count
+    padding = units * piece - rows.shape[0]
+    return jnp.pad(rows, ((0, padding), (0, 0))).reshape(units, piece, width)
 
 
 def half_turn(array):
@@ -618,61 +698,48 @@
     grad_gate, grad_up = activate_back(grad_hidden)
     grad_both = jnp.concatenate([grad_gate, grad_up], axis=1).astype(BF16)
     second_part = dot(grad_both, expand_flat, ((1,), (1,))).astype(BF16)
-    grad_shrink = dot(hidden, grad_rows, ((0,), (0,))).astype(BF16)
-    grad_expand = dot(second, grad_both, ((0,), (0,))).astype(BF16)
-    second_part, grad_shrink, grad_expand = lax.optimization_barrier(
-        (second_part, grad_shrink, grad_expand)
-    )
-    grad_shrink, grad_expand = lax.psum((grad_shrink, grad_expand), "dp")
-    grad_branch, grad_middle, gain_two = exchange(
-        "middle_back_exchange",
-        2,
-        [second_part],
-        [middle, gain_two_row, cotangent],
-        middle_back_step,
-        [
-            jax.ShapeDtypeStruct((local_rows, model_width), BF16),
-            jax.ShapeDtypeStruct((own_rows, model_width), F32),
-            jax.ShapeDtypeStruct((1, model_width), F32),
-        ],
-    )
-    grad_mixed = dot(grad_branch, output_weight, ((1,), (1,))).astype(BF16)
-    dq_t, dk, dv = attend_back(
-        key, key_t, query, query_t, value, grad_mixed, grad_mixed.T, mixed_t, logsum, heads, 256
-    )
-
-    def turn_back(grad):
-        return grad * cosine + dot((grad * sine).astype(BF16), turn, ((1,), (1,)))
-
-    grad_joint = jnp.concatenate([turn_back(dq_t.T), turn_back(dk), dv], axis=1).astype(BF16)
-    first_part = dot(grad_joint, joint_flat, ((1,), (1,)))
-    gain_one = jnp.sum(first_part * first_hat, axis=0, keepdims=True)
-    grad_joint_w = dot(grad_joint, normed, ((0,), (0,)))
-    grad_output = dot(mixed_t, grad_branch)
-    weights = jnp.concatenate([grad_joint_w, grad_output], axis=0).astype(BF16)
-    gains = jnp.concatenate([gain_one, gain_two, jnp.zeros((6, model_width), F32)], axis=0)
+    grad_shrink = dot(hidden, grad_rows, ((0,), (0,)))
+    grad_expand = dot(grad_both, second, ((0,), (0,)))
+    early = jnp.concatenate([grad_shrink, grad_expand], axis=0).astype(BF16)
     shrink_part = dot(hidden, shrink_weight).astype(BF16)
-    grad_tokens, block_out, weights, gains = last_exchange(
-        first_part.astype(BF16),
+    block_out, grad_tokens, early, late, gains = back(
+        second_part,
         shrink_part,
-        to_payload(weights),
-        gains,
+        to_payload(early),
         tokens,
         gain_one_row,
+        gain_two_row,
         middle,
-        grad_middle,
+        cotangent,
+        output_weight,
+        jnp.transpose(joint_weight, (1, 0, 2)),
+        normed,
+        cosine,
+        sine,
+        turn,
+        key,
+        key_t,
+        query,
+        query_t,
+        value,
+        mixed_t,
+        logsum,
+        heads=heads,
+        own=own_rows,
     )
-    weights = weights.reshape(-1, model_width)
-    grad_joint_w = weights[: 3 * inner].astype(F32).T
+    early = early.reshape(-1, model_width)
+    late = late.reshape(-1, model_width)
+    grad_joint_w = late[: 3 * inner].astype(F32).T
+    grad_expand = early[units : 3 * units].astype(F32).T
     return (
         block_out,
         grad_tokens,
         gains[0],
         grad_joint_w.reshape(model_width, 3, inner),
-        weights[3 * inner : 4 * inner].astype(F32),
+        late[3 * inner : 4 * inner].astype(F32),
         gains[1],
-        grad_expand.astype(F32).reshape(model_width, 2, units),
-        grad_shrink.astype(F32),
+        grad_expand.reshape(model_width, 2, units),
+        early[:units].astype(F32),
     )
 
 

time: 234 us -> 196 us (0.84)
  waiting for transfers between devices: 34.3 us -> 0.68 us
  Pallas kernels: 119 us -> 127 us
  matrix products: 26.1 us -> 18.2 us
  local copies, waits for them, and re-layouts: 27.6 us -> 23.9 us
    psum x1 -> x0, waiting for transfers between devices: 33.6 us -> none  [on_device(): grad_shrink, grad_expand = lax.psum((grad_shrink, grad_expand), 'dp')]
    pallas_call x2 -> x1, Pallas kernels: 64.7 us -> 95.3 us  [back(): pl.pallas_call(functools.partial(back_kernel, heads, own, count), in_spec...]
    pallas_call x2 -> x1, Pallas kernels: 46 us -> 23.5 us  [exchange(): pl.pallas_call(functools.partial(exchange_kernel, sums, len(extra), step,...]
    unnamed x83 -> x44, local copies, waits for them, and re-layouts: 18.4 us -> 9.74 us
    dot_general x16 -> x10, matrix products: 26.1 us -> 18.2 us  [dot(): return lax.dot_general(a, b, (dims, ((), ())), preferred_element_type=F32)]
    pallas_call x2 -> x0, local copies, waits for them, and re-layouts: 3.45 us -> none  [attend_back(): pl.pallas_call(functools.partial(attend_back_kernel, heads, per_seq), gri...]
    cos x0 -> x1, local copies, waits for them, and re-layouts: none -> 2.5 us  [rotary_tables(): jnp.cos(angles)]
    sin x0 -> x1, local copies, waits for them, and re-layouts: none -> 2.45 us  [rotary_tables(): jnp.sin(angles)]
  transfers between devices with their start and end apart: 2 -> 1, of which waited for: 1 -> 0; matrix products, arithmetic and copies ran while one was open for 9% -> 14% of each run, Pallas kernels for 37% -> 16%
where the time goes in v3:
time: 196 us
  Pallas kernels  127 us (65%)
  local copies, waits for them, and re-layouts  23.9 us (12%)
  matrix products  18.2 us (9%)
  between operations  14.3 us (7%)
  other arithmetic  11.2 us (6%)
    pallas_call x1, Pallas kernels, back(): pl.pallas_call(functools.partial(back_kernel, heads, own, count), in_spec...  95.3 us
    pallas_call x1, Pallas kernels, exchange(): pl.pallas_call(functools.partial(exchange_kernel, sums, len(extra), step,...  23.5 us
    dot_general x10, matrix products, dot(): return lax.dot_general(a, b, (dims, ((), ())), preferred_element_type=F32)  18.2 us
    unnamed x44, local copies, waits for them, and re-layouts  9.74 us
    pallas_call x1, Pallas kernels, attend(): pl.pallas_call(functools.partial(attend_kernel, heads), grid=(rows // blo...  8.71 us
  transfers between devices with their start and end apart: 1, of which 0 were waited for; matrix products, arithmetic and copies ran while one was open for 14% of the time, Pallas kernels for 16%

profile of v3, /device:TPU:0, one launch (start us, length us, event | category | flops | bytes accessed | tf_op | source)
XLA Modules:
  0.0 195.8 jit_solution(1598270950642362963)
XLA Ops:
  7.2 0.0 copy-start
  7.2 0.0 copy-start.1
  7.2 0.0 all-gather.2.cloned.1.call-start
  7.2 0.7 all-gather.2.cloned.1.call-update
  7.9 1.3 broadcast_in_dim.2.refs_4_
  9.2 1.8 convert_reduce_fusion
  11.0 0.6 fusion.2
  11.6 1.5 copy.28
  13.1 0.6 fusion.33
  13.6 1.2 fusion.21
  14.8 1.2 fusion.22
  16.0 0.5 fusion.4.refs_10_
  16.5 1.7 fusion.8
  18.3 0.9 fusion.26
  19.2 1.0 fusion.37
  20.2 1.0 tile.17
  21.2 2.5 %copy.29.refs_11_ = f32[1024,192]{1,0:T(8,128)} copy(f32[1024,192]{0,1:T(8,128)} %bitcast.64) | data formatting | bytes 1572864 | tf_op jit(solution)/shard_map/cos | solution.py:641
  23.7 1.0 tile.18
  24.6 2.5 %copy.30.refs_12_ = f32[1024,192]{1,0:T(8,128)} copy(f32[1024,192]{0,1:T(8,128)} %bitcast.65) | data formatting | bytes 1572864 | tf_op jit(solution)/shard_map/sin | solution.py:641
  27.1 1.2 copy.26.key.refs_14_
  28.3 2.2 %copy.33.refs_18_ = bf16[1024,192]{1,0:T(8,128)(2,1)} copy(bf16[1024,192]{0,1:T(8,128)(2,1)} %get-tuple-element.28) | data formatting | bytes 786432
  30.5 1.0 copy.32.refs_16_
  31.5 1.0 copy-done.4
  32.5 8.7 %attend.1 = (bf16[192,1024]{1,0:T(8,128)(2,1)S(1)}, f32[8,1024]{1,0:T(8,128)S(1)}) custom-call(bf16[1024,192]{1,0:T(8,128)(2,1)S(1)} %copy.26.key.refs_14_, bf16[192,1024]{1,0:T(8,128)(2,1)S(1)} %bitcast.58, bf16[192,1024]{1,0:T(8,128)(2,1)S(1)} %bitcast.60), custom_call_target="tpu_custom_call" | custom-call | tf_op jit(solution)/shard_map/attend/pallas_call | solution.py:67
  41.2 0.6 copy-done.7
  41.9 0.8 copy-done.5
  42.6 1.6 convolution_convert_fusion.2.refs_0_
  44.2 23.5 %middle_exchange.1 = (bf16[1024,768]{1,0:T(8,128)(2,1)S(1)}, f32[256,768]{1,0:T(8,128)S(1)}) custom-call(bf16[1024,768]{1,0:T(8,128)(2,1)S(1)} %convolution_convert_fusion.2.refs_0_, bf16[1024,768]{1,0:T(8,128)(2,1)S(1)} %copy-done.1, f32[1,768]{1,0:T(1,128)S(1)} %reshape.96.refs_2_.refs_5_), custom_call_target="tpu_custom_call" | custom-call | tf_op jit(solution)/shard_map/middle_exchange/pallas_call | solution.py:238
  67.7 0.0 copy-start.6
  67.7 0.9 copy-done.6
  68.6 1.1 copy-done.9
  69.7 2.5 %fusion.38 = f32[1024,576]{0,1:T(8,128)} fusion(bf16[1024,768]{1,0:T(8,128)(2,1)S(1)} %get-tuple-element.18, bf16[768,576]{0,1:T(8,128)(2,1)S(1)} %bitcast.56), kind=kOutput, calls=%fused_computation.69 | convolution fusion | flops 905969664 | bytes 4816896 | tf_op jit(solution)/shard_map/dot_general | solution.py:25
  72.3 3.6 %fusion.20 = (bf16[1024,288]{0,1:T(8,128)(2,1)S(1)}, bf16[1024,288]{0,1:T(8,128)(2,1)S(1)}, bf16[1024,288]{0,1:T(8,128)(2,1)S(1)}) fusion(f32[1024,576]{0,1:T(8,128)} %fusion.38, bf16[1024,768]{1,0:T(8,128)(2,1)} %all-gather.2.cloned.1.call-done, bf16[288,768]{1,0:T(8,128)(2,1)S(1)} %copy-done.19), kind=kOutput, calls=%fused_computation.32 | convolution fusion | flops 460652544 | bytes 6144000 | tf_op jit(solution)/shard_map/dot_general | solution.py:25
  75.9 1.1 convolution_convert_fusion.3
  77.0 2.6 %convolution_convert_fusion.refs_0_ = bf16[1024,768]{1,0:T(8,128)(2,1)} fusion(bf16[768,576]{0,1:T(8,128)(2,1)S(1)} %bitcast.57, bf16[1024,288]{0,1:T(8,128)(2,1)S(1)} %get-tuple-element.31, bf16[1024,288]{0,1:T(8,128)(2,1)S(1)} %get-tuple-element.30), kind=kOutput, calls=%fused_computation.12 | convolution fusion | flops 909115392 | bytes 3637248 | tf_op jit(solution)/shard_map/dot_general | solution.py:25
  79.6 2.2 %convolution_convert_fusion.1.refs_1_ = bf16[1024,768]{1,0:T(8,128)(2,1)} fusion(bf16[1024,288]{0,1:T(8,128)(2,1)S(1)} %get-tuple-element.32, bf16[288,768]{1,0:T(8,128)(2,1)S(1)} %copy-done.19), kind=kOutput, calls=%fused_computation.13 | convolution fusion | flops 453771264 | bytes 2605056 | tf_op jit(solution)/shard_map/dot_general | solution.py:25
  81.7 0.6 convolution_convert_fusion.4
  82.4 1.3 fusion.7
  83.6 95.3 %back.1 = (bf16[256,768]{1,0:T(8,128)(2,1)}, f32[256,768]{1,0:T(8,128)}, bf16[16,64,768]{2,1,0:T(8,128)(2,1)}, bf16[16,48,768]{2,1,0:T(8,128)(2,1)}, f32[8,768]{1,0:T(8,128)}) custom-call(bf16[1024,768]{1,0:T(8,128)(2,1)} %convolution_convert_fusion.refs_0_, bf16[1024,768]{1,0:T(8,128)(2,1)} %convolution_convert_fusion.1.refs_1_, ...), custom_call_target="tpu_custom_call" | custom-call | tf_op jit(solution)/shard_map/back/pallas_call | solution.py:577
  178.9 1.1 slice.59
  180.0 1.2 slice.58
  181.3 1.0 slice_convert_fusion.2
  182.2 1.3 slice_convert_fusion
  183.6 1.4 slice_reduce_fusion
  185.0 0.9 bitcast_convert_fusion.1
  185.9 1.4 bitcast_convert_fusion
  187.3 0.7 copy.37
  188.0 0.9 copy.38
  (37 shorter events, 0.1 us)
Async XLA Ops:
  7.2 61.4 %copy-start = (bf16[768,2,288]{0,2,1:T(8,128)(2,1)S(1)}, bf16[768,2,288]{0,2,1:T(8,128)(2,1)}, u32[]{:S(2)}) copy-start(bf16[768,2,288]{0,2,1:T(8,128)(2,1)} %param.14) | copy-start | bytes 2654212
  7.2 3.8 %copy-start.1 = (bf16[1024,768]{1,0:T(8,128)(2,1)S(1)}, bf16[1024,768]{1,0:T(8,128)(2,1)}, u32[]{:S(2)}) copy-start(bf16[1024,768]{1,0:T(8,128)(2,1)} %refs_3_.1) | copy-start | bytes 4718596
  7.2 65.1 %all-gather.2.cloned.1.call-start = ((), (), s32[]{:S(2)}) async-start(), calls=%async_computation | async-start | bytes 1966080 | tf_op jit(solution)/shard_map/all_gather | solution.py:665
  9.2 2.4 %copy-start.12 = (bf16[768,3,192]{0,2,1:T(8,128)(2,1)S(1)}, bf16[768,3,192]{0,2,1:T(8,128)(2,1)}, u32[]{:S(2)}) copy-start(bf16[768,3,192]{0,2,1:T(8,128)(2,1)} %param.11) | copy-start | bytes 2654212
  11.6 4.4 %copy-start.16 = (f32[768]{0:T(1024)S(1)}, f32[768]{0:T(1024)}, u32[]{:S(2)}) copy-start(f32[768]{0:T(1024)} %param.10) | copy-start | bytes 9220
  16.5 1.7 copy-start.11
  19.2 1.0 copy-start.17
  20.2 11.4 %copy-start.2 = (bf16[1024,192]{0,1:T(8,128)(2,1)}, bf16[1024,192]{0,1:T(8,128)(2,1)S(1)}, u32[]{:S(2)}) copy-start(bf16[1024,192]{0,1:T(8,128)(2,1)S(1)} %get-tuple-element.29) | copy-start | bytes 1179652
  20.2 24.0 %copy-start.8 = (f32[1,768]{1,0:T(1,128)}, f32[1,768]{1,0:T(1,128)S(1)}, u32[]{:S(2)}) copy-start(f32[1,768]{1,0:T(1,128)S(1)} %reshape.96.refs_2_.refs_5_) | copy-start | bytes 9220
  28.3 12.9 %copy-start.3 = (bf16[1024,192]{1,0:T(8,128)(2,1)}, bf16[1024,192]{1,0:T(8,128)(2,1)S(1)}, u32[]{:S(2)}) copy-start(bf16[1024,192]{1,0:T(8,128)(2,1)S(1)} %copy.26.key.refs_14_) | copy-start | bytes 1179652
  31.5 1.0 copy-start.4
  41.2 0.6 copy-start.7
  41.8 0.8 copy-start.5
  67.7 0.9 copy-start.6
  68.6 1.1 copy-start.9
  69.7 2.5 %copy-start.19 = (bf16[288,768]{1,0:T(8,128)(2,1)S(1)}, bf16[288,768]{1,0:T(8,128)(2,1)}, u32[]{:S(2)}) copy-start(bf16[288,768]{1,0:T(8,128)(2,1)} %param.15) | copy-start | bytes 1327108
  72.3 3.6 %copy-start.10 = (bf16[1024,768]{1,0:T(8,128)(2,1)S(1)}, bf16[1024,768]{1,0:T(8,128)(2,1)}, u32[]{:S(2)}) copy-start(bf16[1024,768]{1,0:T(8,128)(2,1)} %copy-done.9) | copy-start | bytes 4718596
  79.6 2.2 %copy-start.18 = (bf16[1024,768]{1,0:T(8,128)(2,1)S(1)}, bf16[1024,768]{1,0:T(8,128)(2,1)}, u32[]{:S(2)}) copy-start(bf16[1024,768]{1,0:T(8,128)(2,1)} %all-gather.2.cloned.1.call-done) | copy-start | bytes 4718596
  178.9 2.3 %copy-start.13 = (bf16[16,64,768]{2,1,0:T(8,128)(2,1)S(1)}, bf16[16,64,768]{2,1,0:T(8,128)(2,1)}, u32[]{:S(2)}) copy-start(bf16[16,64,768]{2,1,0:T(8,128)(2,1)} %get-tuple-element.25) | copy-start | bytes 4718596
  185.0 2.3 %copy-start.15 = (bf16[256,768]{1,0:T(8,128)(2,1)S(1)}, bf16[256,768]{1,0:T(8,128)(2,1)}, u32[]{:S(2)}) copy-start(bf16[256,768]{1,0:T(8,128)(2,1)} %get-tuple-element.43) | copy-start | bytes 1179652
  185.9 2.1 %copy-start.14 = (f32[256,768]{1,0:T(8,128)S(1)}, f32[256,768]{1,0:T(8,128)}, u32[]{:S(2)}) copy-start(f32[256,768]{1,0:T(8,128)} %get-tuple-element.44) | copy-start | bytes 2359300
Sparse Core Ops, SparseCore 0:
  9.6 22.3 all-gather.1

commit v4 on v3

--- a/solution.py
+++ b/solution.py
@@ -48,41 +48,6 @@
 def head_columns(array, head):
     index = lax.broadcasted_iota(jnp.int32, array.shape, 1) // HEAD_DIM
     return jnp.where(index == head, array, jnp.zeros_like(array))
-
-
-def attend_kernel(heads, key, query_t, value_t, mixed_t, logsum):
-    for head in range(heads):
-        rows = slice(head * HEAD_DIM, (head + 1) * HEAD_DIM)
-        scores = dot(key[...], head_rows(query_t[...], head))
-        peak = jnp.max(scores, axis=0, keepdims=True)
-        exps = jnp.exp(scores - peak)
-        total = jnp.sum(exps, axis=0, keepdims=True)
-        mixed_t[rows, :] = (dot(value_t[rows, :], exps.astype(BF16)) * (1.0 / total)).astype(BF16)
-        logsum[head : head + 1, :] = peak + jnp.log(total)
-
-
-def attend(key, query_t, value_t, heads, block):
-    width, rows = query_t.shape
-    per_seq = SEQ_LEN // block
-    return pl.pallas_call(
-        functools.partial(attend_kernel, heads),
-        grid=(rows // block,),
-        in_specs=[
-            pl.BlockSpec((SEQ_LEN, width), lambda i: (i // per_seq, 0)),
-            pl.BlockSpec((width, block), lambda i: (0, i)),
-            pl.BlockSpec((width, SEQ_LEN), lambda i: (0, i // per_seq)),
-        ],
-        out_specs=[
-            pl.BlockSpec((width, block), lambda i: (0, i)),
-            pl.BlockSpec((8, block), lambda i: (0, i)),
-        ],
-        out_shape=[
-            jax.ShapeDtypeStruct((width, rows), BF16),
-            jax.ShapeDtypeStruct((8, rows), F32),
-        ],
-        compiler_params=pltpu.CompilerParams(vmem_limit_bytes=VMEM_LIMIT),
-        name="attend",
-    )(key, query_t, value_t)
 
 
 def remote(src, dst, send_sem, recv_sem, target):
@@ -143,18 +108,29 @@
         return copy
 
     def start(self):
-        self.onward, self.mine, self.sideways = {}, {}, {}
-        for first, kept, owner in ((0, self.onward, self.cross), (1, self.mine, self.core_peer)):
-            for slot, part in enumerate(self.parts):
-                for chunk in range(CHUNKS):
-                    kept[slot, chunk] = self.to_core(
-                        part.at[self.at(owner, chunk)],
-                        self.from_core.at[2 * slot + first, self.here(chunk)],
-                        2 * slot + first,
-                        chunk,
-                    )
+        self.start_onward()
+        self.start_mine()
+
+    def start_onward(self):
+        self.onward = self.send_block(0, self.cross)
+
+    def start_mine(self):
+        self.mine = self.send_block(1, self.core_peer)
+
+    def send_block(self, first, owner):
+        return {
+            (slot, chunk): self.to_core(
+                part.at[self.at(owner, chunk)],
+                self.from_core.at[2 * slot + first, self.here(chunk)],
+                2 * slot + first,
+                chunk,
+            )
+            for slot, part in enumerate(self.parts)
+            for chunk in range(CHUNKS)
+        }
 
     def cross_over(self):
+        self.sideways = {}
         for slot, part in enumerate(self.parts):
             for chunk in range(CHUNKS):
                 here = self.here(chunk)
@@ -207,17 +183,6 @@
             copy.wait_send()
 
 
-def exchange_kernel(sums, extras, step, own, *refs):
-    work = GroupSum(refs[:sums], own, True, refs[-7:])
-    greet(work.peers())
-    work.start()
-    work.cross_over()
-    outs = refs[sums + extras : -7]
-    work.totals(step, refs[sums : sums + extras], outs)
-    work.spread(outs[0])
-    work.close()
-
-
 def exchange_scratch(sums, own, width, gather):
     core_slots = 2 * sums + (2 if gather else 0)
     side_slots = sums + (1 if gather else 0)
@@ -232,20 +197,90 @@
     ]
 
 
-def exchange(name, number, parts, extra, step, out_shape):
-    own = parts[0].shape[0] // 4
-    sums = len(parts)
+def front_kernel(heads, own, *refs):
+    tokens, gain_one, gain_two, joint, output_weight, cosine, sine = refs[:7]
+    second, middle, normed, key, key_t, query, query_t, value, mixed_t, logsum = refs[7:17]
+    value_t, branch_part = refs[17:19]
+    group = GroupSum((branch_part,), own, True, refs[19:])
+    greet(group.peers())
+    rows = tokens.shape[0]
+
+    def project(number, carry):
+        down = pl.ds(pl.multiple_of(number * own, own), own)
+        hat, _ = norm_parts(tokens[down, :].astype(F32))
+        normal = (hat * gain_one[...]).astype(BF16)
+        normed[down, :] = normal
+        cos, sin = cosine[down, :], sine[down, :]
+        turned = (dot(normal, joint[0]) * cos + dot(normal, joint[3]) * sin) * SCALE
+        query[down, :] = turned.astype(BF16)
+        query_t[:, down] = turned.T.astype(BF16)
+        turned = dot(normal, joint[1]) * cos + dot(normal, joint[4]) * sin
+        key[down, :] = turned.astype(BF16)
+        key_t[:, down] = turned.T.astype(BF16)
+        plain = dot(normal, joint[2])
+        value[down, :] = plain.astype(BF16)
+        value_t[:, down] = plain.T.astype(BF16)
+        return carry
+
+    lax.fori_loop(0, rows // own, project, 0)
+
+    def attend(owner):
+        down = pl.ds(pl.multiple_of(owner * own, own), own)
+        for head in range(heads):
+            part = slice(head * HEAD_DIM, (head + 1) * HEAD_DIM)
+            scores = dot(key[...], head_rows(query_t[:, down], head))
+            peak = jnp.max(scores, axis=0, keepdims=True)
+            exps = jnp.exp(scores - peak)
+            total = jnp.sum(exps, axis=0, keepdims=True)
+            mixed = dot(value_t[part, :], exps.astype(BF16)) * (1.0 / total)
+            mixed_t[part, down] = mixed.astype(BF16)
+            logsum[head : head + 1, down] = peak + jnp.log(total)
+        branch = dot(mixed_t[:, down], output_weight[...], ((0,), (0,)))
+        branch_part[down, :] = branch.astype(BF16)
+
+    attend(group.cross)
+    group.start_onward()
+    attend(group.side_peer)
+    group.cross_over()
+    attend(group.core_peer)
+    group.start_mine()
+    attend(group.me)
+    group.totals(middle_step, (tokens, gain_two), (second, middle))
+    group.spread(second)
+    group.close()
+
+
+def front(tokens, *rest, heads, own):
+    rows, width = tokens.shape
+    inner = heads * HEAD_DIM
+    down, across = (rows, inner), (inner, rows)
+    shapes = [
+        ((rows, width), BF16),
+        ((own, width), F32),
+        ((rows, width), BF16),
+        (down, BF16),
+        (across, BF16),
+        (down, BF16),
+        (across, BF16),
+        (down, BF16),
+        (across, BF16),
+        ((8, rows), F32),
+    ]
     return pl.pallas_call(
-        functools.partial(exchange_kernel, sums, len(extra), step, own),
-        in_specs=[VMEM] * (sums + len(extra)),
-        out_specs=[VMEM] * len(out_shape),
-        out_shape=out_shape,
-        scratch_shapes=exchange_scratch(sums, own, parts[0].shape[1], True),
+        functools.partial(front_kernel, heads, own),
+        in_specs=[VMEM] * 7,
+        out_specs=[VMEM] * 10,
+        out_shape=[jax.ShapeDtypeStruct(*shape) for shape in shapes],
+        scratch_shapes=[
+            pltpu.VMEM(across, BF16),
+            pltpu.VMEM((rows, width), BF16),
+            *exchange_scratch(1, own, width, True),
+        ],
         compiler_params=pltpu.CompilerParams(
-            collective_id=number, has_side_effects=True, vmem_limit_bytes=VMEM_LIMIT
+            collective_id=1, has_side_effects=True, vmem_limit_bytes=VMEM_LIMIT
         ),
-        name=name,
-    )(*parts, *extra)
+        name="front",
+    )(tokens, *rest)
 
 
 def middle_step(chunk, rows, here, totals, extra, outs):
@@ -289,6 +324,7 @@
         self.waves, self.count = WAVES, payload.shape[0] // (2 * WAVES)
         data = lax.axis_index("dp")
         self.outer, self.inner = data // 2, data % 2
+        self.near, self.spread, self.shared = {}, {}, {}
         self.unsent = []
 
     def pair(self):
@@ -322,20 +358,15 @@
     def hops(self):
         return [*range(1, self.count), 0]
 
-    def start(self):
-        self.near = {
-            (wave, hop): self.to_pair(
+    def start(self, wave):
+        for hop in self.hops():
+            self.near[wave, hop] = self.to_pair(
                 self.payload.at[self.unit(wave, 1 - self.inner, self.place(hop))],
                 self.from_pair.at[wave, hop],
                 0,
                 wave,
                 hop,
             )
-            for wave in range(self.waves)
-            for hop in self.hops()
-        }
-        self.spread = {}
-        self.shared = {}
 
     def scatter(self, wave):
         for hop in self.hops():
@@ -466,7 +497,8 @@
     greet(norm_sum.peers() + [{"tensor": norm_sum.cross}] + early.peers())
 
     norm_sum.start()
-    early.start()
+    early.start(0)
+    early.start(1)
     norm_sum.cross_over()
     early.scatter(0)
     norm_sum.totals(
@@ -480,6 +512,9 @@
     out_sum.start()
     early.collect(1)
 
+    late_step = inner // late_part.shape[1]
+    grad_output = dot(mixed_t[...], grad_branch[...]).astype(BF16)
+    late_part[:late_step] = grad_output.reshape((late_step,) + late_part.shape[1:])
     grad_mixed[...] = dot(grad_branch[...], output_weight[...], ((1,), (1,))).astype(BF16)
     grad_mixed_t[...] = dot(output_weight[...], grad_branch[...], ((1,), (1,))).astype(BF16)
     dk[...] = jnp.zeros_like(dk)
@@ -516,6 +551,24 @@
         return (grad * cosine[...] + moved).astype(BF16)
 
     grad_parts = (turn_back(dq_t[...].T[:, :inner]), turn_back(dk[...]), dv[...].astype(BF16))
+    units, piece, _ = late_part.shape
+    step = inner // piece
+    whole = units == 4 * step
+
+    def keep(place, weight):
+        kept = weight.astype(BF16).reshape(step, piece, width)
+        late_part[place * step : (place + 1) * step] = kept
+
+    if not whole:
+        late_part[4 * step :] = jnp.zeros((units - 4 * step, piece, width), BF16)
+    keep(1, dot(grad_parts[2], normed[...], ((0,), (0,))))
+    if whole:
+        late.start(0)
+    keep(2, dot(grad_parts[0], normed[...], ((0,), (0,))))
+    keep(3, dot(grad_parts[1], normed[...], ((0,), (0,))))
+    if not whole:
+        late.start(0)
+    late.start(1)
     gain_term = jnp.zeros((1, width), F32)
     for owner in range(rows // own):
         here = slice(owner * own, (owner + 1) * own)
@@ -529,30 +582,19 @@
     terms[0:1, :] = gain_term / gain_one[...]
     terms[1:2, :] = term_two[...]
     gain.start()
-
-    units, piece, _ = late_part.shape
-    step = inner // piece
-    for part in range(3):
-        grad_weight = dot(grad_parts[part], normed[...], ((0,), (0,))).astype(BF16)
-        late_part[part * step : (part + 1) * step] = grad_weight.reshape(step, piece, width)
-    grad_output = dot(mixed_t[...], grad_branch[...]).astype(BF16)
-    late_part[3 * step : 4 * step] = grad_output.reshape(step, piece, width)
-    if units > 4 * step:
-        late_part[4 * step :] = jnp.zeros((units - 4 * step, piece, width), BF16)
-    late.start()
+    late.scatter(0)
     token_sum.cross_over()
     gain.pair_up()
-    out_sum.totals(out_step, (middle,), (block_out,))
-    early.finish()
-    late.scatter(0)
     late.scatter(1)
     late.collect(0)
+    out_sum.totals(out_step, (middle,), (block_out,))
     gain.spread()
     late.collect(1)
     token_sum.totals(token_step, (tokens, gain_one, grad_middle), (grad_tokens,))
     late.relay(0)
     late.relay(1)
     gain.finish()
+    early.finish()
     late.finish()
     for work in (norm_sum, out_sum, token_sum, early, late, gain):
         work.close()
@@ -634,11 +676,10 @@
 
 def rotary_tables(rows, heads):
     half_width = HEAD_DIM // 2
-    frequency = THETA ** (-(jnp.arange(half_width, dtype=F32) * 2.0 / HEAD_DIM))
-    angles = jnp.arange(SEQ_LEN, dtype=F32)[:, None] * frequency[None, :]
-    angles = jnp.tile(angles, (1, 2 * heads))
-    repeat = rows // SEQ_LEN
-    return jnp.tile(jnp.cos(angles), (repeat, 1)), jnp.tile(jnp.sin(angles), (repeat, 1))
+    frequency = THETA ** (-(np.arange(half_width) * 2.0 / HEAD_DIM))
+    angles = (np.arange(rows) % SEQ_LEN)[:, None] * frequency[None, :]
+    angles = np.tile(angles, (1, 2 * heads))
+    return jnp.asarray(np.cos(angles), F32), jnp.asarray(np.sin(angles), F32)
 
 
 def on_device(
@@ -656,7 +697,6 @@
     heads = joint_weight.shape[2] // HEAD_DIM
     inner = heads * HEAD_DIM
     units = expand_weight.shape[2]
-    joint_flat = joint_weight.reshape(model_width, 3 * inner)
     expand_flat = expand_weight.reshape(model_width, 2 * units)
     gain_one_row = first_gain.reshape(1, model_width)
     gain_two_row = second_gain.reshape(1, model_width)
@@ -664,28 +704,19 @@
 
     grad_rows = lax.all_gather(cotangent, "tensor", axis=0, tiled=True)
 
-    first_hat, _ = norm_parts(tokens.astype(F32))
-    normed = (first_hat * first_gain).astype(BF16)
-    turned = [dot(joint_weight[:, part], turn).astype(BF16) for part in (0, 1)]
-    joint = dot(normed, jnp.concatenate([joint_flat, *turned], axis=1))
+    joint_parts = jnp.transpose(joint_weight, (1, 0, 2))
+    turned = [dot(joint_parts[part], turn).astype(BF16)[None] for part in (0, 1)]
     cosine, sine = rotary_tables(local_rows, heads)
-    query = (joint[:, :inner] * cosine + joint[:, 3 * inner : 4 * inner] * sine).astype(BF16)
-    query = query * jnp.asarray(SCALE, BF16)
-    key = (joint[:, inner : 2 * inner] * cosine + joint[:, 4 * inner :] * sine).astype(BF16)
-    value = joint[:, 2 * inner : 3 * inner].astype(BF16)
-    query_t, key_t, value_t = query.T, key.T, value.T
-    mixed_t, logsum = attend(key, query_t, value_t, heads, 256)
-    branch_part = dot(mixed_t, output_weight, ((0,), (0,))).astype(BF16)
-    second, middle = exchange(
-        "middle_exchange",
-        1,
-        [branch_part],
-        [tokens, gain_two_row],
-        middle_step,
-        [
-            jax.ShapeDtypeStruct((local_rows, model_width), BF16),
-            jax.ShapeDtypeStruct((own_rows, model_width), F32),
-        ],
+    second, middle, normed, key, key_t, query, query_t, value, mixed_t, logsum = front(
+        tokens,
+        gain_one_row,
+        gain_two_row,
+        jnp.concatenate([joint_parts, *turned], axis=0),
+        output_weight,
+        cosine,
+        sine,
+        heads=heads,
+        own=own_rows,
     )
     gate_up = dot(second, expand_flat)
 
@@ -712,7 +743,7 @@
         middle,
         cotangent,
         output_weight,
-        jnp.transpose(joint_weight, (1, 0, 2)),
+        joint_parts,
         normed,
         cosine,
         sine,
@@ -729,14 +760,17 @@
     )
     early = early.reshape(-1, model_width)
     late = late.reshape(-1, model_width)
-    grad_joint_w = late[: 3 * inner].astype(F32).T
+    grad_value_w, grad_query_w, grad_key_w = (
+        late[part * inner : (part + 1) * inner] for part in (1, 2, 3)
+    )
+    grad_joint_w = jnp.concatenate([grad_query_w, grad_key_w, grad_value_w], axis=0).astype(F32).T
     grad_expand = early[units : 3 * units].astype(F32).T
     return (
         block_out,
         grad_tokens,
         gains[0],
         grad_joint_w.reshape(model_width, 3, inner),
-        late[3 * inner : 4 * inner].astype(F32),
+        late[:inner].astype(F32),
         gains[1],
         grad_expand.reshape(model_width, 2, units),
         early[:units].astype(F32),

time: 196 us -> 184 us (0.939)
  local copies, waits for them, and re-layouts: 23.9 us -> 13.1 us
  Pallas kernels: 127 us -> 131 us
  matrix products: 18.2 us -> 14.9 us
    pallas_call x2 -> x1, Pallas kernels: 32.2 us -> 36.2 us  [front(): pl.pallas_call(functools.partial(front_kernel, heads, own), in_specs=[VME...]
    dot_general x10 -> x8, matrix products: 18.2 us -> 14.9 us  [dot(): return lax.dot_general(a, b, (dims, ((), ())), preferred_element_type=F32)]
    cos x1 -> x0, local copies, waits for them, and re-layouts: 2.5 us -> none  [rotary_tables(): jnp.cos(angles)]
    sin x1 -> x0, local copies, waits for them, and re-layouts: 2.45 us -> none  [rotary_tables(): jnp.sin(angles)]
    reduce_sum x2 -> x0, other arithmetic: 2.36 us -> none  [the longest x1 1.76 us: norm_parts(): centred = values - jnp.mean(values, axis=-1, keepdims=True)]
    slice x2 -> x1, local copies, waits for them, and re-layouts: 2.33 us -> 0.08 us  [on_device(): late[:inner].astype(F32)]
    unnamed x44 -> x47, local copies, waits for them, and re-layouts: 9.74 us -> 9.82 us
  transfers between devices with their start and end apart: 1 -> 1, of which waited for: 0 -> 0; matrix products, arithmetic and copies ran while one was open for 14% -> 5% of each run, Pallas kernels for 16% -> 20%
where the time goes in v4:
time: 184 us; the launch traced here: 183 us
  Pallas kernels  131 us (71%)
  matrix products  14.9 us (8%)
  between operations  14.2 us (8%)
  local copies, waits for them, and re-layouts  13.1 us (7%)
  other arithmetic  9.76 us (5%)
    pallas_call x1, Pallas kernels, back(): pl.pallas_call(functools.partial(back_kernel, heads, own, count), in_spec...  94.4 us
    pallas_call x1, Pallas kernels, front(): pl.pallas_call(functools.partial(front_kernel, heads, own), in_specs=[VME...  36.2 us
    dot_general x8, matrix products, dot(): return lax.dot_general(a, b, (dims, ((), ())), preferred_element_type=F32)  14.9 us
    unnamed x47, local copies, waits for them, and re-layouts  9.82 us
  transfers between devices with their start and end apart: 1, of which 0 were waited for; matrix products, arithmetic and copies ran while one was open for 5% of the time, Pallas kernels for 20%

profile of v4, /device:TPU:0, one launch (start us, length us, event | category | flops | bytes accessed | tf_op | source)
XLA Modules:
  0.0 183.3 jit_solution(8214973908507025199)
XLA Ops:
  7.2 0.0 copy-start
  7.2 0.0 copy-start.16
  7.2 0.0 all-gather.2.cloned.1.call-start
  7.2 0.7 all-gather.2.cloned.1.call-update
  7.9 0.7 reshape.50.refs_1_.refs_4_
  8.6 0.7 reshape.51.refs_2_.refs_5_
  9.3 1.5 copy.22
  10.8 0.0 copy-start.14
  10.9 0.0 copy-done.16
  10.9 0.3 convolution_convert_fusion.4
  11.2 0.2 copy.24
  11.3 0.3 convolution_convert_fusion.5
  11.6 0.2 copy.23
  11.8 0.0 copy-start.1
  11.8 0.0 copy-start.2
  11.9 0.0 copy-start.3
  11.9 1.7 pad_maximum_fusion.refs_3_
  13.6 0.0 copy-done.12
  13.6 0.0 copy-done.1
  13.6 0.2 copy-done.2
  13.8 0.3 copy-done.3
  14.0 36.2 %front.1 = (bf16[1024,768]{1,0:T(8,128)(2,1)}, f32[256,768]{1,0:T(8,128)S(1)}, bf16[1024,768]{1,0:T(8,128)(2,1)}, bf16[1024,192]{1,0:T(8,128)(2,1)S(1)}, bf16[19...) custom-call(bf16[1024,768]{1,0:T(8,128)(2,1)} %refs_3_.1, ...), custom_call_target="tpu_custom_call" | custom-call | tf_op jit(solution)/shard_map/front/pallas_call | solution.py:269
  50.3 0.0 copy-start.4
  50.3 0.9 copy-done.4
  51.1 0.8 copy-done.5
  51.9 0.8 copy-done.6
  52.7 0.8 copy-done.7
  53.6 0.7 copy-done.8
  54.3 0.8 copy-done.9
  55.1 0.7 copy-done.10
  55.8 0.6 copy-done.11
  56.4 4.0 %fusion.13 = f32[1024,576]{0,1:T(8,128)} fusion(bf16[1024,768]{1,0:T(8,128)(2,1)} %get-tuple-element.23, bf16[768,576]{0,1:T(8,128)(2,1)S(1)} %bitcast.40), kind=kOutput, calls=%fused_computation.35 | convolution fusion | flops 905969664 | bytes 4816896 | tf_op jit(solution)/shard_map/dot_general | solution.py:25
  60.5 3.6 %fusion.9 = (bf16[1024,288]{0,1:T(8,128)(2,1)S(1)}, bf16[1024,288]{0,1:T(8,128)(2,1)S(1)}, bf16[1024,288]{0,1:T(8,128)(2,1)S(1)}) fusion(f32[1024,576]{0,1:T(8,128)} %fusion.13, bf16[1024,768]{1,0:T(8,128)(2,1)} %all-gather.2.cloned.1.call-done, bf16[288,768]{1,0:T(8,128)(2,1)S(1)} %copy-done.21), kind=kOutput, calls=%fused_computation.19 | convolution fusion | flops 460652544 | bytes 6144000 | tf_op jit(solution)/shard_map/dot_general | solution.py:25
  64.1 1.1 convolution_convert_fusion.2
  65.2 2.8 %convolution_convert_fusion.refs_0_ = bf16[1024,768]{1,0:T(8,128)(2,1)} fusion(bf16[768,576]{0,1:T(8,128)(2,1)S(1)} %bitcast.41, bf16[1024,288]{0,1:T(8,128)(2,1)S(1)} %get-tuple-element.41, bf16[1024,288]{0,1:T(8,128)(2,1)S(1)} %get-tuple-element.40), kind=kOutput, calls=%fused_computation.6 | convolution fusion | flops 909115392 | bytes 3637248 | tf_op jit(solution)/shard_map/dot_general | solution.py:25
  68.0 2.2 %convolution_convert_fusion.1.refs_1_ = bf16[1024,768]{1,0:T(8,128)(2,1)} fusion(bf16[1024,288]{0,1:T(8,128)(2,1)S(1)} %get-tuple-element.42, bf16[288,768]{1,0:T(8,128)(2,1)S(1)} %copy-done.21), kind=kOutput, calls=%fused_computation.7 | convolution fusion | flops 453771264 | bytes 2605056 | tf_op jit(solution)/shard_map/dot_general | solution.py:25
  70.2 0.6 convolution_convert_fusion.3
  70.8 1.3 fusion.2
  72.0 94.4 %back.1 = (bf16[256,768]{1,0:T(8,128)(2,1)}, f32[256,768]{1,0:T(8,128)}, bf16[16,64,768]{2,1,0:T(8,128)(2,1)}, bf16[16,48,768]{2,1,0:T(8,128)(2,1)}, f32[8,768]{1,0:T(8,128)}) custom-call(bf16[1024,768]{1,0:T(8,128)(2,1)} %convolution_convert_fusion.refs_0_, bf16[1024,768]{1,0:T(8,128)(2,1)} %convolution_convert_fusion.1.refs_1_, ...), custom_call_target="tpu_custom_call" | custom-call | tf_op jit(solution)/shard_map/back/pallas_call | solution.py:619
  166.5 2.0 %slice_convert_fusion.1 = f32[288,768]{1,0:T(8,128)} fusion(bf16[1024,768]{1,0:T(8,128)(2,1)} %bitcast.54), kind=kLoop, calls=%fused_computation.26 | loop fusion | flops 221184 | bytes 1327104 | tf_op jit(solution)/shard_map/convert_element_type | solution.py:776
  168.5 2.6 %slice_convert_fusion = f32[576,768]{1,0:T(8,128)} fusion(bf16[1024,768]{1,0:T(8,128)(2,1)} %bitcast.55), kind=kLoop, calls=%fused_computation.24 | loop fusion | flops 442368 | bytes 2654208 | tf_op jit(solution)/shard_map/reshape | solution.py:775
  171.1 1.4 slice_reduce_fusion
  172.5 0.1 fusion.12
  172.6 0.9 bitcast_convert_fusion
  173.5 1.3 maximum_convert_fusion
  174.8 0.7 copy.27
  175.6 0.0 copy-done.17
  175.6 0.9 copy.28
  (24 shorter events, 0.0 us)
Async XLA Ops:
  7.2 49.3 %copy-start = (bf16[768,2,288]{0,2,1:T(8,128)(2,1)S(1)}, bf16[768,2,288]{0,2,1:T(8,128)(2,1)}, u32[]{:S(2)}) copy-start(bf16[768,2,288]{0,2,1:T(8,128)(2,1)} %param.16) | copy-start | bytes 2654212
  7.2 3.7 %copy-start.16 = (bf16[192,192]{1,0:T(8,128)(2,1)S(1)}, bf16[192,192]{1,0:T(8,128)(2,1)}, u32[]{:S(2)}) copy-start(bf16[192,192]{1,0:T(8,128)(2,1)} %constant.21.clone.refs_13_) | copy-start | bytes 221188
  7.2 53.3 %all-gather.2.cloned.1.call-start = ((), (), s32[]{:S(2)}) async-start(), calls=%async_computation | async-start | bytes 1966080 | tf_op jit(solution)/shard_map/all_gather | solution.py:705
  8.6 5.0 %copy-start.12 = (f32[1,768]{1,0:T(1,128)}, f32[1,768]{1,0:T(1,128)S(1)}, u32[]{:S(2)}) copy-start(f32[1,768]{1,0:T(1,128)S(1)} %reshape.50.refs_1_.refs_4_) | copy-start | bytes 9220
  9.3 4.3 %copy-start.13 = (f32[1,768]{1,0:T(1,128)}, f32[1,768]{1,0:T(1,128)S(1)}, u32[]{:S(2)}) copy-start(f32[1,768]{1,0:T(1,128)S(1)} %reshape.51.refs_2_.refs_5_) | copy-start | bytes 9220
  10.8 2.7 %copy-start.14 = (bf16[768,3,192]{2,0,1:T(8,128)(2,1)}, bf16[768,3,192]{2,0,1:T(8,128)(2,1)S(1)}, u32[]{:S(2)}) copy-start(bf16[768,3,192]{2,0,1:T(8,128)(2,1)S(1)} %copy.22) | copy-start | bytes 2654212
  11.8 1.8 copy-start.1
  11.8 1.9 %copy-start.2 = (f32[1024,192]{1,0:T(8,128)S(1)}, f32[1024,192]{1,0:T(8,128)}, u32[]{:S(2)}) copy-start(f32[1024,192]{1,0:T(8,128)} %constant.22.clone.refs_5_.refs_11_) | copy-start | bytes 2359300
  11.9 2.2 %copy-start.3 = (bf16[192,768]{1,0:T(8,128)(2,1)S(1)}, bf16[192,768]{1,0:T(8,128)(2,1)}, u32[]{:S(2)}) copy-start(bf16[192,768]{1,0:T(8,128)(2,1)} %refs_8_.1) | copy-start | bytes 884740
  50.3 0.9 copy-start.4
  51.1 0.8 copy-start.5
  51.9 0.8 copy-start.6
  52.7 0.8 copy-start.7
  53.6 0.7 copy-start.8
  54.3 0.8 copy-start.9
  55.1 0.8 copy-start.10
  55.8 0.6 copy-start.11
  56.4 4.0 %copy-start.21 = (bf16[288,768]{1,0:T(8,128)(2,1)S(1)}, bf16[288,768]{1,0:T(8,128)(2,1)}, u32[]{:S(2)}) copy-start(bf16[288,768]{1,0:T(8,128)(2,1)} %param.17) | copy-start | bytes 1327108
  60.5 3.6 %copy-start.20 = (bf16[1024,768]{1,0:T(8,128)(2,1)S(1)}, bf16[1024,768]{1,0:T(8,128)(2,1)}, u32[]{:S(2)}) copy-start(bf16[1024,768]{1,0:T(8,128)(2,1)} %get-tuple-element.23) | copy-start | bytes 4718596
  68.0 2.2 %copy-start.19 = (bf16[1024,768]{1,0:T(8,128)(2,1)S(1)}, bf16[1024,768]{1,0:T(8,128)(2,1)}, u32[]{:S(2)}) copy-start(bf16[1024,768]{1,0:T(8,128)(2,1)} %all-gather.2.cloned.1.call-done) | copy-start | bytes 4718596
  168.5 4.0 %copy-start.15 = (bf16[16,48,768]{2,1,0:T(8,128)(2,1)S(1)}, bf16[16,48,768]{2,1,0:T(8,128)(2,1)}, u32[]{:S(2)}) copy-start(bf16[16,48,768]{2,1,0:T(8,128)(2,1)} %get-tuple-element.36) | copy-start | bytes 3538948
  172.6 2.2 %copy-start.18 = (bf16[256,768]{1,0:T(8,128)(2,1)S(1)}, bf16[256,768]{1,0:T(8,128)(2,1)}, u32[]{:S(2)}) copy-start(bf16[256,768]{1,0:T(8,128)(2,1)} %get-tuple-element.55) | copy-start | bytes 1179652
  173.5 2.1 %copy-start.17 = (f32[256,768]{1,0:T(8,128)S(1)}, f32[256,768]{1,0:T(8,128)}, u32[]{:S(2)}) copy-start(f32[256,768]{1,0:T(8,128)} %get-tuple-element.56) | copy-start | bytes 2359300
Sparse Core Ops, SparseCore 0:
  9.6 23.4 all-gather.1

commit v5 on v4

--- a/solution.py
+++ b/solution.py
@@ -506,11 +506,9 @@
         (middle, gain_two, cotangent),
         (grad_branch, grad_middle, term_two),
     )
+    norm_sum.spread(grad_branch)
     early.scatter(1)
-    early.collect(0)
-    norm_sum.spread(grad_branch)
     out_sum.start()
-    early.collect(1)
 
     late_step = inner // late_part.shape[1]
     grad_output = dot(mixed_t[...], grad_branch[...]).astype(BF16)
@@ -519,6 +517,7 @@
     grad_mixed_t[...] = dot(output_weight[...], grad_branch[...], ((1,), (1,))).astype(BF16)
     dk[...] = jnp.zeros_like(dk)
     dv[...] = jnp.zeros_like(dv)
+    early.collect(0)
 
     def attend_rows(number, carry):
         down = pl.ds(pl.multiple_of(number * block, block), block)
@@ -542,9 +541,9 @@
     blocks = rows // block
     lax.fori_loop(0, blocks // 2, attend_rows, 0)
     out_sum.cross_over()
+    early.collect(1)
+    lax.fori_loop(blocks // 2, blocks, attend_rows, 0)
     early.relay(0)
-    lax.fori_loop(blocks // 2, blocks, attend_rows, 0)
-    early.relay(1)
 
     def turn_back(grad):
         moved = dot((grad * sine[...]).astype(BF16), turn[...], ((1,), (1,)))
@@ -578,6 +577,7 @@
         first_part[here, :] = value_rows.astype(BF16)
         gain_term += jnp.sum(value_rows * normed[here, :].astype(F32), axis=0, keepdims=True)
     token_sum.start()
+    early.relay(1)
     terms[...] = jnp.zeros_like(terms)
     terms[0:1, :] = gain_term / gain_one[...]
     terms[1:2, :] = term_two[...]

time: 184 us -> 185 us (level)
  no operation moved by 1% of the time
where the time goes in v5:
time: 185 us; the launch traced here: 184 us
  Pallas kernels  131 us (71%)
  matrix products  14.9 us (8%)
  between operations  14.2 us (8%)
  local copies, waits for them, and re-layouts  13.1 us (7%)
  other arithmetic  9.76 us (5%)
    pallas_call x1, Pallas kernels, back(): pl.pallas_call(functools.partial(back_kernel, heads, own, count), in_spec...  95.3 us
    pallas_call x1, Pallas kernels, front(): pl.pallas_call(functools.partial(front_kernel, heads, own), in_specs=[VME...  36.2 us
    dot_general x8, matrix products, dot(): return lax.dot_general(a, b, (dims, ((), ())), preferred_element_type=F32)  14.9 us
    unnamed x47, local copies, waits for them, and re-layouts  9.82 us
  transfers between devices with their start and end apart: 1, of which 0 were waited for; matrix products, arithmetic and copies ran while one was open for 5% of the time, Pallas kernels for 20%

profile of v5, /device:TPU:0, one launch (start us, length us, event | category | flops | bytes accessed | tf_op | source)
XLA Modules:
  0.0 184.1 jit_solution(15106317147525975868)
XLA Ops:
  7.2 0.0 copy-start
  7.2 0.0 copy-start.16
  7.2 0.0 all-gather.2.cloned.1.call-start
  7.2 0.7 all-gather.2.cloned.1.call-update
  7.9 0.7 reshape.50.refs_1_.refs_4_
  8.6 0.7 reshape.51.refs_2_.refs_5_
  9.3 1.5 copy.22
  10.8 0.0 copy-start.14
  10.9 0.0 copy-done.16
  10.9 0.3 convolution_convert_fusion.4
  11.2 0.2 copy.24
  11.3 0.3 convolution_convert_fusion.5
  11.6 0.2 copy.23
  11.8 0.0 copy-start.1
  11.8 0.0 copy-start.2
  11.9 0.0 copy-start.3
  11.9 1.7 pad_maximum_fusion.refs_3_
  13.6 0.0 copy-done.12
  13.6 0.0 copy-done.14
  13.6 0.2 copy-done.2
  13.8 0.3 copy-done.3
  14.0 36.2 %front.1 = (bf16[1024,768]{1,0:T(8,128)(2,1)}, f32[256,768]{1,0:T(8,128)S(1)}, bf16[1024,768]{1,0:T(8,128)(2,1)}, bf16[1024,192]{1,0:T(8,128)(2,1)S(1)}, bf16[19...) custom-call(bf16[1024,768]{1,0:T(8,128)(2,1)} %refs_3_.1, ...), custom_call_target="tpu_custom_call" | custom-call | tf_op jit(solution)/shard_map/front/pallas_call | solution.py:269
  50.3 0.0 copy-start.4
  50.3 0.9 copy-done.4
  51.1 0.8 copy-done.5
  51.9 0.8 copy-done.6
  52.7 0.8 copy-done.7
  53.6 0.7 copy-done.8
  54.3 0.8 copy-done.9
  55.1 0.7 copy-done.10
  55.8 0.6 copy-done.11
  56.4 4.0 %fusion.13 = f32[1024,576]{0,1:T(8,128)} fusion(bf16[1024,768]{1,0:T(8,128)(2,1)} %get-tuple-element.23, bf16[768,576]{0,1:T(8,128)(2,1)S(1)} %bitcast.40), kind=kOutput, calls=%fused_computation.35 | convolution fusion | flops 905969664 | bytes 4816896 | tf_op jit(solution)/shard_map/dot_general | solution.py:25
  60.5 3.6 %fusion.9 = (bf16[1024,288]{0,1:T(8,128)(2,1)S(1)}, bf16[1024,288]{0,1:T(8,128)(2,1)S(1)}, bf16[1024,288]{0,1:T(8,128)(2,1)S(1)}) fusion(f32[1024,576]{0,1:T(8,128)} %fusion.13, bf16[1024,768]{1,0:T(8,128)(2,1)} %all-gather.2.cloned.1.call-done, bf16[288,768]{1,0:T(8,128)(2,1)S(1)} %copy-done.21), kind=kOutput, calls=%fused_computation.19 | convolution fusion | flops 460652544 | bytes 6144000 | tf_op jit(solution)/shard_map/dot_general | solution.py:25
  64.1 1.1 convolution_convert_fusion.2
  65.2 2.8 %convolution_convert_fusion.refs_0_ = bf16[1024,768]{1,0:T(8,128)(2,1)} fusion(bf16[768,576]{0,1:T(8,128)(2,1)S(1)} %bitcast.41, bf16[1024,288]{0,1:T(8,128)(2,1)S(1)} %get-tuple-element.41, bf16[1024,288]{0,1:T(8,128)(2,1)S(1)} %get-tuple-element.40), kind=kOutput, calls=%fused_computation.6 | convolution fusion | flops 909115392 | bytes 3637248 | tf_op jit(solution)/shard_map/dot_general | solution.py:25
  68.0 2.2 %convolution_convert_fusion.1.refs_1_ = bf16[1024,768]{1,0:T(8,128)(2,1)} fusion(bf16[1024,288]{0,1:T(8,128)(2,1)S(1)} %get-tuple-element.42, bf16[288,768]{1,0:T(8,128)(2,1)S(1)} %copy-done.21), kind=kOutput, calls=%fused_computation.7 | convolution fusion | flops 453771264 | bytes 2605056 | tf_op jit(solution)/shard_map/dot_general | solution.py:25
  70.2 0.6 convolution_convert_fusion.3
  70.8 1.3 fusion.2
  72.0 95.3 %back.1 = (bf16[256,768]{1,0:T(8,128)(2,1)}, f32[256,768]{1,0:T(8,128)}, bf16[16,64,768]{2,1,0:T(8,128)(2,1)}, bf16[16,48,768]{2,1,0:T(8,128)(2,1)}, f32[8,768]{1,0:T(8,128)}) custom-call(bf16[1024,768]{1,0:T(8,128)(2,1)} %convolution_convert_fusion.refs_0_, bf16[1024,768]{1,0:T(8,128)(2,1)} %convolution_convert_fusion.1.refs_1_, ...), custom_call_target="tpu_custom_call" | custom-call | tf_op jit(solution)/shard_map/back/pallas_call | solution.py:619
  167.3 2.0 %slice_convert_fusion.1 = f32[288,768]{1,0:T(8,128)} fusion(bf16[1024,768]{1,0:T(8,128)(2,1)} %bitcast.54), kind=kLoop, calls=%fused_computation.26 | loop fusion | flops 221184 | bytes 1327104 | tf_op jit(solution)/shard_map/convert_element_type | solution.py:776
  169.3 2.6 %slice_convert_fusion = f32[576,768]{1,0:T(8,128)} fusion(bf16[1024,768]{1,0:T(8,128)(2,1)} %bitcast.55), kind=kLoop, calls=%fused_computation.24 | loop fusion | flops 442368 | bytes 2654208 | tf_op jit(solution)/shard_map/reshape | solution.py:775
  171.9 1.4 slice_reduce_fusion
  173.3 0.1 fusion.12
  173.4 0.9 bitcast_convert_fusion
  174.3 1.3 maximum_convert_fusion
  175.6 0.0 copy-done.18
  175.6 0.7 copy.27
  176.4 0.9 copy.28
  (24 shorter events, 0.0 us)
Async XLA Ops:
  7.2 49.3 %copy-start = (bf16[768,2,288]{0,2,1:T(8,128)(2,1)S(1)}, bf16[768,2,288]{0,2,1:T(8,128)(2,1)}, u32[]{:S(2)}) copy-start(bf16[768,2,288]{0,2,1:T(8,128)(2,1)} %param.16) | copy-start | bytes 2654212
  7.2 3.7 %copy-start.16 = (bf16[192,192]{1,0:T(8,128)(2,1)S(1)}, bf16[192,192]{1,0:T(8,128)(2,1)}, u32[]{:S(2)}) copy-start(bf16[192,192]{1,0:T(8,128)(2,1)} %constant.21.clone.refs_13_) | copy-start | bytes 221188
  7.2 53.3 %all-gather.2.cloned.1.call-start = ((), (), s32[]{:S(2)}) async-start(), calls=%async_computation | async-start | bytes 1966080 | tf_op jit(solution)/shard_map/all_gather | solution.py:705
  8.6 5.0 %copy-start.12 = (f32[1,768]{1,0:T(1,128)}, f32[1,768]{1,0:T(1,128)S(1)}, u32[]{:S(2)}) copy-start(f32[1,768]{1,0:T(1,128)S(1)} %reshape.50.refs_1_.refs_4_) | copy-start | bytes 9220
  9.3 4.3 %copy-start.13 = (f32[1,768]{1,0:T(1,128)}, f32[1,768]{1,0:T(1,128)S(1)}, u32[]{:S(2)}) copy-start(f32[1,768]{1,0:T(1,128)S(1)} %reshape.51.refs_2_.refs_5_) | copy-start | bytes 9220
  10.8 2.7 %copy-start.14 = (bf16[768,3,192]{2,0,1:T(8,128)(2,1)}, bf16[768,3,192]{2,0,1:T(8,128)(2,1)S(1)}, u32[]{:S(2)}) copy-start(bf16[768,3,192]{2,0,1:T(8,128)(2,1)S(1)} %copy.22) | copy-start | bytes 2654212
  11.8 1.8 copy-start.1
  11.8 1.9 %copy-start.2 = (f32[1024,192]{1,0:T(8,128)S(1)}, f32[1024,192]{1,0:T(8,128)}, u32[]{:S(2)}) copy-start(f32[1024,192]{1,0:T(8,128)} %constant.22.clone.refs_5_.refs_11_) | copy-start | bytes 2359300
  11.9 2.2 %copy-start.3 = (bf16[192,768]{1,0:T(8,128)(2,1)S(1)}, bf16[192,768]{1,0:T(8,128)(2,1)}, u32[]{:S(2)}) copy-start(bf16[192,768]{1,0:T(8,128)(2,1)} %refs_8_.1) | copy-start | bytes 884740
  50.3 0.9 copy-start.4
  51.1 0.8 copy-start.5
  51.9 0.8 copy-start.6
  52.7 0.8 copy-start.7
  53.6 0.7 copy-start.8
  54.3 0.8 copy-start.9
  55.1 0.8 copy-start.10
  55.8 0.6 copy-start.11
  56.4 4.0 %copy-start.21 = (bf16[288,768]{1,0:T(8,128)(2,1)S(1)}, bf16[288,768]{1,0:T(8,128)(2,1)}, u32[]{:S(2)}) copy-start(bf16[288,768]{1,0:T(8,128)(2,1)} %param.17) | copy-start | bytes 1327108
  60.5 3.6 %copy-start.20 = (bf16[1024,768]{1,0:T(8,128)(2,1)S(1)}, bf16[1024,768]{1,0:T(8,128)(2,1)}, u32[]{:S(2)}) copy-start(bf16[1024,768]{1,0:T(8,128)(2,1)} %get-tuple-element.23) | copy-start | bytes 4718596
  68.0 2.2 %copy-start.19 = (bf16[1024,768]{1,0:T(8,128)(2,1)S(1)}, bf16[1024,768]{1,0:T(8,128)(2,1)}, u32[]{:S(2)}) copy-start(bf16[1024,768]{1,0:T(8,128)(2,1)} %all-gather.2.cloned.1.call-done) | copy-start | bytes 4718596
  169.3 4.0 %copy-start.15 = (bf16[16,48,768]{2,1,0:T(8,128)(2,1)S(1)}, bf16[16,48,768]{2,1,0:T(8,128)(2,1)}, u32[]{:S(2)}) copy-start(bf16[16,48,768]{2,1,0:T(8,128)(2,1)} %get-tuple-element.36) | copy-start | bytes 3538948
  173.4 2.2 %copy-start.18 = (bf16[256,768]{1,0:T(8,128)(2,1)S(1)}, bf16[256,768]{1,0:T(8,128)(2,1)}, u32[]{:S(2)}) copy-start(bf16[256,768]{1,0:T(8,128)(2,1)} %get-tuple-element.55) | copy-start | bytes 1179652
  174.3 2.1 %copy-start.17 = (f32[256,768]{1,0:T(8,128)S(1)}, f32[256,768]{1,0:T(8,128)}, u32[]{:S(2)}) copy-start(f32[256,768]{1,0:T(8,128)} %get-tuple-element.56) | copy-start | bytes 2359300
Sparse Core Ops, SparseCore 0:
  9.6 23.4 all-gather.1
